TPU v7x, 512 devices: a whole 4x8x8 slice. The times are simulated.
512 devices in a mesh: blk: 32 (over x, z), uly: 4 (over y_lo, core), rep: 4 (over y_hi).
Axes of the slice: x: 4, y: 8 (y_hi: 4, y_lo: 2; y = y_hi * 2 + y_lo), z: 8, core: 2. Of those that a mesh axis runs over, the one named last changes fastest.
Arguments:
- queries: bfloat16 [65536, 1536], P(('rep', 'blk', 'uly')), parts along dimension 0, may hold values from -13 to 13
- key_input: bfloat16 [65536, 1536], P(('rep', 'blk', 'uly')), parts along dimension 0, may hold values from -5 to 5
- value_input: bfloat16 [65536, 1536], P(('rep', 'blk', 'uly')), parts along dimension 0, may hold values from -6 to 6
- grad_out: bfloat16 [65536, 1536], P(('rep', 'blk', 'uly')), parts along dimension 0, may hold values from -6 to 6
- keep_index: int32 [8192], P(('rep', 'blk', 'uly')), parts along dimension 0, may hold values from 0 to 16383, as said below
Outputs:
- grad_q: bfloat16 [65536, 1536], P(('rep', 'blk', 'uly')), parts along dimension 0
- grad_k: bfloat16 [65536, 1536], P(('rep', 'blk', 'uly')), parts along dimension 0
- grad_v: bfloat16 [65536, 1536], P(('rep', 'blk', 'uly')), parts along dimension 0
There are 4 independent parts, one for each index of `rep`. A program takes and returns all parts, laid end to end along the dimension named above; each array names one. Nothing has to cross between parts.
Inputs may be any that keep to these rules, and one draw needn't show every extreme that they name: keep_index[j] lies in its cell, 8 * j to 8 * j + 7; the first and the last cell keep their outermost token.
All inputs are finite; a program needn't handle non-finite values.
Results may differ from a plain program's by a relative error of at most 0.035.
Values may be sent and summed in bfloat16 or wider, within the bound.
A program may use at most 64 MiB of HBM per device.

v0:
```python
import math

import jax
import jax.numpy as jnp
from jax import lax
from jax.sharding import PartitionSpec as P

HEAD_DIM = 128


very_low = -1e30


def shifted(array, axis, by):
    size = lax.axis_size(axis)
    return lax.ppermute(array, axis, [(i, (i + by) % size) for i in range(size)])


def head_view(rows):
    return rows.reshape(rows.shape[0], rows.shape[1] // HEAD_DIM, HEAD_DIM)


def row_view(blocks):
    return blocks.reshape(blocks.shape[0], blocks.shape[1] * blocks.shape[2])


def online_block(running, query_heads, key_block, value_block, score_scale):
    running_top, running_total, running_sum = running
    key_heads = head_view(key_block)
    value_heads = head_view(value_block)
    scores = (
        jnp.einsum("qhd,khd->hqk", query_heads, key_heads, preferred_element_type=jnp.float32)
        * score_scale
    )
    fresh_top = jnp.maximum(running_top, jnp.max(scores, axis=2))
    factor = jnp.exp(running_top - fresh_top)
    weights = jnp.exp(scores - fresh_top[:, :, None])
    running_total = running_total * factor + jnp.sum(weights, axis=2)
    running_sum = running_sum * factor[:, :, None] + jnp.einsum(
        "hqk,khd->hqd",
        weights.astype(jnp.bfloat16),
        value_heads,
        preferred_element_type=jnp.float32,
    )
    return (fresh_top, running_total, running_sum)


def fold_keys(running, query_heads, key_rows, value_rows, score_scale):
    row_count = key_rows.shape[0]
    block_rows = math.gcd(row_count, 512)
    blocks = row_count // block_rows
    row_width = key_rows.shape[1]
    key_stack = key_rows.reshape(blocks, block_rows, row_width)
    value_stack = value_rows.reshape(blocks, block_rows, row_width)

    def visit(state, block_pair):
        return (online_block(state, query_heads, block_pair[0], block_pair[1], score_scale), None)

    result, unused = lax.scan(visit, running, (key_stack, value_stack))
    return result


def backward_block(query_heads, grad_heads, log_total, row_delta, pair, score_scale):
    key_heads = head_view(pair[0])
    value_heads = head_view(pair[1])
    scores = (
        jnp.einsum("qhd,khd->hqk", query_heads, key_heads, preferred_element_type=jnp.float32)
        * score_scale
    )
    probs = jnp.exp(scores - log_total[:, :, None])
    dprobs = jnp.einsum("qhd,khd->hqk", grad_heads, value_heads, preferred_element_type=jnp.float32)
    dscores = (probs * (dprobs - row_delta[:, :, None])).astype(jnp.bfloat16)
    query_add = jnp.einsum("hqk,khd->qhd", dscores, key_heads, preferred_element_type=jnp.float32)
    key_add = jnp.einsum("hqk,qhd->khd", dscores, query_heads, preferred_element_type=jnp.float32)
    value_add = jnp.einsum(
        "hqk,qhd->khd", probs.astype(jnp.bfloat16), grad_heads, preferred_element_type=jnp.float32
    )
    return (query_add, jnp.stack([row_view(key_add), row_view(value_add)]))


def pass_keys(pair):
    return shifted(pair, "blk", 1)


def pass_grads(grad_pair):
    return shifted(grad_pair, "blk", 1)


def per_device(queries, key_input, value_input, grad_out, keep_index):
    tok_dev = queries.shape[0]
    local_rows = keep_index % tok_dev
    key_pair = jnp.stack(
        [jnp.take(key_input, local_rows, axis=0), jnp.take(value_input, local_rows, axis=0)]
    )
    query_pair = jnp.stack([queries, grad_out])
    query_pair = lax.all_to_all(query_pair, "uly", split_axis=2, concat_axis=1, tiled=True)
    key_pair = lax.all_to_all(key_pair, "uly", split_axis=2, concat_axis=1, tiled=True)
    query_heads = head_view(query_pair[0])
    grad_heads = head_view(query_pair[1])
    score_scale = HEAD_DIM ** (-0.5)
    query_count = query_heads.shape[0]
    head_count = query_heads.shape[1]
    start_state = (
        jnp.full((head_count, query_count), very_low, jnp.float32),
        jnp.zeros((head_count, query_count), jnp.float32),
        jnp.zeros((head_count, query_count, HEAD_DIM), jnp.float32),
    )
    piece = lax.all_gather(key_pair, "blk", axis=1, tiled=True)
    running = fold_keys(start_state, query_heads, piece[0], piece[1], score_scale)
    running_top, running_total, running_sum = running
    log_total = running_top + jnp.log(running_total)
    attended = (running_sum / running_total[:, :, None]).astype(jnp.bfloat16)
    row_delta = jnp.einsum("hqd,qhd->hq", attended, grad_heads, preferred_element_type=jnp.float32)
    cycle_size = lax.axis_size("blk")
    zero_grads = jnp.zeros(key_pair.shape, jnp.float32)
    zero_query = jnp.zeros(query_heads.shape, jnp.float32)

    def block_grads(pair):
        return backward_block(query_heads, grad_heads, log_total, row_delta, pair, score_scale)

    def cycle_turn(turn_index, carried):
        pair, grad_acc, query_acc = carried
        query_add, pair_add = block_grads(pair)
        return (pass_keys(pair), pass_grads(grad_acc + pair_add), query_acc + query_add)

    unused, grad_acc, query_acc = lax.fori_loop(
        0, cycle_size, cycle_turn, (key_pair, zero_grads, zero_query)
    )
    pair_scale = jnp.array([score_scale, 1.0], jnp.float32)[:, None, None]
    query_grads = row_view(query_acc * score_scale).astype(jnp.bfloat16)
    pair_grads = (grad_acc * pair_scale).astype(jnp.bfloat16)
    query_back = lax.all_to_all(query_grads, "uly", split_axis=0, concat_axis=1, tiled=True)
    pair_back = lax.all_to_all(pair_grads, "uly", split_axis=1, concat_axis=2, tiled=True)
    blank = jnp.zeros((tok_dev, queries.shape[1]), jnp.bfloat16)
    return (
        query_back,
        blank.at[local_rows].set(pair_back[0]),
        blank.at[local_rows].set(pair_back[1]),
    )


def solution(mesh):
    in_specs = (
        P(("rep", "blk", "uly"), None),
        P(("rep", "blk", "uly"), None),
        P(("rep", "blk", "uly"), None),
        P(("rep", "blk", "uly"), None),
        P(("rep", "blk", "uly")),
    )
    out_specs = (
        P(("rep", "blk", "uly"), None),
        P(("rep", "blk", "uly"), None),
        P(("rep", "blk", "uly"), None),
    )
    return jax.shard_map(
        per_device, mesh=mesh, in_specs=in_specs, out_specs=out_specs, check_vma=False
    )
```

profile of v0, /device:TPU:1, one launch (start us, length us, event | category | flops | bytes accessed | tf_op | source)
XLA Modules:
  0.0 658.6 jit_solution(5859155075774053892)
XLA Ops:
  11.9 12.6 %all_to_all.64 = bf16[4,2,6144]{2,1,0:T(2,128)(2,1)S(1)} all-to-all(bf16[4,2,6144]{2,1,0:T(2,128)(2,1)S(1)} %reshape.96), channel_id=1, replica_groups=mesh['blk'=32,'uly'=4,'rep'=4] {'uly'}, dimensions={0} | all-to-all | bytes 196608 | tf_op jit(solution)/shard_map/all_to_all | solution.py:97
  28.5 4.4 all-to-all-start.1
  33.0 10.8 %all-to-all-done.1 = bf16[2,128,1536]{1,0,2:T(2,128)(2,1)S(1)} async-done(((bf16[2,128,1536]{1,0,2:T(2,128)(2,1)}), bf16[2,128,1536]{1,0,2:T(2,128)(2,1)S(1)}, u32[]{:S(2)}, u32[]{:S(2)}) %all-to-all-start.1) | async-done | bytes 786464 | tf_op jit(solution)/shard_map/all_to_all | solution.py:96
  46.8 61.6 %all-gather.2.cloned.1.call-done = bf16[2,2048,384]{2,1,0:T(8,128)(2,1)} async-done(((bf16[2,64,384]{2,1,0:T(8,128)(2,1)}), bf16[2,2048,384]{2,1,0:T(8,128)(2,1)}) %all-gather.2.cloned.1.call-update) | async-done | bytes 3145744 | tf_op jit(solution)/shard_map/all_gather | solution.py:108
  108.4 3.9 fusion.28
  112.3 49.9 %while.30 = (s32[]{:T(128)}, f32[3,512]{1,0:T(4,128)S(1)}, f32[3,512]{1,0:T(4,128)}, f32[3,512,128]{2,1,0:T(8,128)}, bf16[4,512,384]{2,1,0:T(8,128)(2,1)}, /*ind...) while((s32[]{:T(128)}, f32[3,512]{1,0:T(4,128)S(1)}, ...), condition=%wide.region_3.5_spmd.clone, body=%wide.region_0.0_spmd.clone.sunk | while | flops 409542144 | bytes 15433837 | solution.py:59
  168.3 446.2 %while.31 = (s32[]{:T(128)}, bf16[2,64,384]{2,1,0:T(8,128)(2,1)S(1)}, f32[2,64,384]{2,1,0:T(8,128)S(1)}, f32[512,3,128]{2,0,1:T(8,128)S(1)}, bf16[512,3,128]{2,0...) while((s32[]{:T(128)}, ...), condition=%wide.region_5.7_spmd.clone, body=%wide.region_4.6_spmd.clone.sunk | while | flops 126910464 | bytes 8417471 | solution.py:126
  177.1 6.6 collective-permute-done.1
  192.3 5.3 collective-permute-done.1
  206.3 5.0 collective-permute-done.1
  220.0 4.3 collective-permute-done.1
  230.0 3.1 collective-permute-done
  233.0 4.3 collective-permute-done.1
  243.0 3.1 collective-permute-done
  246.0 4.3 collective-permute-done.1
  256.0 3.1 collective-permute-done
  259.1 4.3 collective-permute-done.1
  269.0 4.4 collective-permute-done
  285.1 4.4 collective-permute-done.1
  295.1 3.2 collective-permute-done
  298.3 5.4 collective-permute-done.1
  309.3 4.2 collective-permute-done
  313.5 5.4 collective-permute-done.1
  324.5 3.1 collective-permute-done
  327.6 5.6 collective-permute-done.1
  338.8 3.1 collective-permute-done
  341.9 4.7 collective-permute-done.1
  352.2 3.1 collective-permute-done
  355.3 5.0 collective-permute-done.1
  369.0 5.4 collective-permute-done.1
  380.0 3.1 collective-permute-done
  383.1 5.4 collective-permute-done.1
  394.1 3.1 collective-permute-done
  397.1 5.4 collective-permute-done.1
  411.2 5.4 collective-permute-done.1
  422.2 3.1 collective-permute-done
  425.3 5.4 collective-permute-done.1
  439.3 5.4 collective-permute-done.1
  450.3 3.1 collective-permute-done
  453.4 5.4 collective-permute-done.1
  464.4 3.1 collective-permute-done
  467.5 5.4 collective-permute-done.1
  481.6 5.5 collective-permute-done.1
  492.7 3.1 collective-permute-done
  495.8 5.5 collective-permute-done.1
  506.9 3.1 collective-permute-done
  509.9 5.5 collective-permute-done.1
  521.0 3.1 collective-permute-done
  524.1 5.5 collective-permute-done.1
  535.2 3.1 collective-permute-done
  538.3 5.5 collective-permute-done.1
  549.4 3.1 collective-permute-done
  552.4 5.5 collective-permute-done.1
  563.5 3.1 collective-permute-done
  566.6 5.5 collective-permute-done.1
  577.7 3.1 collective-permute-done
  580.8 5.5 collective-permute-done.1
  591.9 3.1 collective-permute-done
  594.9 5.5 collective-permute-done.1
  606.0 3.1 collective-permute-done
  609.1 5.5 collective-permute-done.1
  615.4 21.1 %all-to-all-start.3 = ((bf16[2,64,384]{2,0,1:T(2,128)(2,1)}), bf16[2,64,384]{2,0,1:T(2,128)(2,1)S(1)}, u32[]{:S(2)}, u32[]{:S(2)}) async-start(bf16[2,64,384]{2,0,1:T(2,128)(2,1)} %copy.116), calls=%async_computation.3 | async-start | bytes 196608 | tf_op jit(solution)/shard_map/all_to_all | solution.py:133
  639.9 4.4 all-to-all-start.2
  647.7 3.1 all-to-all-done.2
  (626 shorter events, 283.3 us)
Async XLA Ops:
  7.2 101.2 %all-gather.2.cloned.1.call-start = ((), (), s32[]{:S(2)}) async-start(), calls=%async_computation.4 | async-start | bytes 3244032 | tf_op jit(solution)/shard_map/all_gather | solution.py:108
  28.5 15.2 %all-to-all-start.1 = ((bf16[2,128,1536]{1,0,2:T(2,128)(2,1)}), bf16[2,128,1536]{1,0,2:T(2,128)(2,1)S(1)}, u32[]{:S(2)}, u32[]{:S(2)}) async-start(bf16[2,128,1536]{1,0,2:T(2,128)(2,1)} %copy.107), calls=%async_computation.1 | async-start | bytes 1572864 | tf_op jit(solution)/shard_map/all_to_all | solution.py:96
  168.4 8.7 %collective-permute-start = (bf16[2,64,384]{2,1,0:T(8,128)(2,1)S(1)}, bf16[2,64,384]{2,1,0:T(8,128)(2,1)S(1)}, u32[]{:S(2)}, u32[]{:S(2)}) collective-permute-start(bf16[2,64,384]{2,1,0:T(8,128)(2,1)S(1)} %copy.171), channel_id=1, source_target_pairs={{0,16},{16,32},{32,48},{48,64},{64,80},{80,96},{96,112},{112,128},... | collective-permute-start | bytes 294920 | tf_op jit(solution)/shard_map/while/body/eval_jaxpr/ppermute | solution.py:16
  172.5 11.1 %collective-permute-start.1 = (f32[2,64,384]{2,1,0:T(8,128)S(1)}, f32[2,64,384]{2,1,0:T(8,128)S(1)}, u32[]{:S(2)}, u32[]{:S(2)}) collective-permute-start(f32[2,64,384]{2,1,0:T(8,128)S(1)} %maximum_add_fusion.2), channel_id=1, source_target_pairs={{0,16},{16,32},{32,48},{48,64},{64,80},{80,96},{96,112},{112,128},... | collective-permute-start | bytes 589832 | tf_op jit(solution)/shard_map/while/body/eval_jaxpr/ppermute | solution.py:16
  183.6 8.7 %collective-permute-start = (bf16[2,64,384]{2,1,0:T(8,128)(2,1)S(1)}, bf16[2,64,384]{2,1,0:T(8,128)(2,1)S(1)}, u32[]{:S(2)}, u32[]{:S(2)}) collective-permute-start(bf16[2,64,384]{2,1,0:T(8,128)(2,1)S(1)} %copy.171), channel_id=1, source_target_pairs={{0,16},{16,32},{32,48},{48,64},{64,80},{80,96},{96,112},{112,128},... | collective-permute-start | bytes 294920 | tf_op jit(solution)/shard_map/while/body/eval_jaxpr/ppermute | solution.py:16
  186.9 10.7 %collective-permute-start.1 = (f32[2,64,384]{2,1,0:T(8,128)S(1)}, f32[2,64,384]{2,1,0:T(8,128)S(1)}, u32[]{:S(2)}, u32[]{:S(2)}) collective-permute-start(f32[2,64,384]{2,1,0:T(8,128)S(1)} %maximum_add_fusion.2), channel_id=1, source_target_pairs={{0,16},{16,32},{32,48},{48,64},{64,80},{80,96},{96,112},{112,128},... | collective-permute-start | bytes 589832 | tf_op jit(solution)/shard_map/while/body/eval_jaxpr/ppermute | solution.py:16
  197.6 8.7 %collective-permute-start = (bf16[2,64,384]{2,1,0:T(8,128)(2,1)S(1)}, bf16[2,64,384]{2,1,0:T(8,128)(2,1)S(1)}, u32[]{:S(2)}, u32[]{:S(2)}) collective-permute-start(bf16[2,64,384]{2,1,0:T(8,128)(2,1)S(1)} %copy.171), channel_id=1, source_target_pairs={{0,16},{16,32},{32,48},{48,64},{64,80},{80,96},{96,112},{112,128},... | collective-permute-start | bytes 294920 | tf_op jit(solution)/shard_map/while/body/eval_jaxpr/ppermute | solution.py:16
  200.9 10.4 %collective-permute-start.1 = (f32[2,64,384]{2,1,0:T(8,128)S(1)}, f32[2,64,384]{2,1,0:T(8,128)S(1)}, u32[]{:S(2)}, u32[]{:S(2)}) collective-permute-start(f32[2,64,384]{2,1,0:T(8,128)S(1)} %maximum_add_fusion.2), channel_id=1, source_target_pairs={{0,16},{16,32},{32,48},{48,64},{64,80},{80,96},{96,112},{112,128},... | collective-permute-start | bytes 589832 | tf_op jit(solution)/shard_map/while/body/eval_jaxpr/ppermute | solution.py:16
  211.3 8.7 %collective-permute-start = (bf16[2,64,384]{2,1,0:T(8,128)(2,1)S(1)}, bf16[2,64,384]{2,1,0:T(8,128)(2,1)S(1)}, u32[]{:S(2)}, u32[]{:S(2)}) collective-permute-start(bf16[2,64,384]{2,1,0:T(8,128)(2,1)S(1)} %copy.171), channel_id=1, source_target_pairs={{0,16},{16,32},{32,48},{48,64},{64,80},{80,96},{96,112},{112,128},... | collective-permute-start | bytes 294920 | tf_op jit(solution)/shard_map/while/body/eval_jaxpr/ppermute | solution.py:16
  214.6 9.7 %collective-permute-start.1 = (f32[2,64,384]{2,1,0:T(8,128)S(1)}, f32[2,64,384]{2,1,0:T(8,128)S(1)}, u32[]{:S(2)}, u32[]{:S(2)}) collective-permute-start(f32[2,64,384]{2,1,0:T(8,128)S(1)} %maximum_add_fusion.2), channel_id=1, source_target_pairs={{0,16},{16,32},{32,48},{48,64},{64,80},{80,96},{96,112},{112,128},... | collective-permute-start | bytes 589832 | tf_op jit(solution)/shard_map/while/body/eval_jaxpr/ppermute | solution.py:16
  224.3 8.7 %collective-permute-start = (bf16[2,64,384]{2,1,0:T(8,128)(2,1)S(1)}, bf16[2,64,384]{2,1,0:T(8,128)(2,1)S(1)}, u32[]{:S(2)}, u32[]{:S(2)}) collective-permute-start(bf16[2,64,384]{2,1,0:T(8,128)(2,1)S(1)} %copy.171), channel_id=1, source_target_pairs={{0,16},{16,32},{32,48},{48,64},{64,80},{80,96},{96,112},{112,128},... | collective-permute-start | bytes 294920 | tf_op jit(solution)/shard_map/while/body/eval_jaxpr/ppermute | solution.py:16
  227.6 9.7 %collective-permute-start.1 = (f32[2,64,384]{2,1,0:T(8,128)S(1)}, f32[2,64,384]{2,1,0:T(8,128)S(1)}, u32[]{:S(2)}, u32[]{:S(2)}) collective-permute-start(f32[2,64,384]{2,1,0:T(8,128)S(1)} %maximum_add_fusion.2), channel_id=1, source_target_pairs={{0,16},{16,32},{32,48},{48,64},{64,80},{80,96},{96,112},{112,128},... | collective-permute-start | bytes 589832 | tf_op jit(solution)/shard_map/while/body/eval_jaxpr/ppermute | solution.py:16
  237.4 8.7 %collective-permute-start = (bf16[2,64,384]{2,1,0:T(8,128)(2,1)S(1)}, bf16[2,64,384]{2,1,0:T(8,128)(2,1)S(1)}, u32[]{:S(2)}, u32[]{:S(2)}) collective-permute-start(bf16[2,64,384]{2,1,0:T(8,128)(2,1)S(1)} %copy.171), channel_id=1, source_target_pairs={{0,16},{16,32},{32,48},{48,64},{64,80},{80,96},{96,112},{112,128},... | collective-permute-start | bytes 294920 | tf_op jit(solution)/shard_map/while/body/eval_jaxpr/ppermute | solution.py:16
  240.6 9.7 %collective-permute-start.1 = (f32[2,64,384]{2,1,0:T(8,128)S(1)}, f32[2,64,384]{2,1,0:T(8,128)S(1)}, u32[]{:S(2)}, u32[]{:S(2)}) collective-permute-start(f32[2,64,384]{2,1,0:T(8,128)S(1)} %maximum_add_fusion.2), channel_id=1, source_target_pairs={{0,16},{16,32},{32,48},{48,64},{64,80},{80,96},{96,112},{112,128},... | collective-permute-start | bytes 589832 | tf_op jit(solution)/shard_map/while/body/eval_jaxpr/ppermute | solution.py:16
  250.4 8.7 %collective-permute-start = (bf16[2,64,384]{2,1,0:T(8,128)(2,1)S(1)}, bf16[2,64,384]{2,1,0:T(8,128)(2,1)S(1)}, u32[]{:S(2)}, u32[]{:S(2)}) collective-permute-start(bf16[2,64,384]{2,1,0:T(8,128)(2,1)S(1)} %copy.171), channel_id=1, source_target_pairs={{0,16},{16,32},{32,48},{48,64},{64,80},{80,96},{96,112},{112,128},... | collective-permute-start | bytes 294920 | tf_op jit(solution)/shard_map/while/body/eval_jaxpr/ppermute | solution.py:16
  253.7 9.7 %collective-permute-start.1 = (f32[2,64,384]{2,1,0:T(8,128)S(1)}, f32[2,64,384]{2,1,0:T(8,128)S(1)}, u32[]{:S(2)}, u32[]{:S(2)}) collective-permute-start(f32[2,64,384]{2,1,0:T(8,128)S(1)} %maximum_add_fusion.2), channel_id=1, source_target_pairs={{0,16},{16,32},{32,48},{48,64},{64,80},{80,96},{96,112},{112,128},... | collective-permute-start | bytes 589832 | tf_op jit(solution)/shard_map/while/body/eval_jaxpr/ppermute | solution.py:16
  263.4 10.0 %collective-permute-start = (bf16[2,64,384]{2,1,0:T(8,128)(2,1)S(1)}, bf16[2,64,384]{2,1,0:T(8,128)(2,1)S(1)}, u32[]{:S(2)}, u32[]{:S(2)}) collective-permute-start(bf16[2,64,384]{2,1,0:T(8,128)(2,1)S(1)} %copy.171), channel_id=1, source_target_pairs={{0,16},{16,32},{32,48},{48,64},{64,80},{80,96},{96,112},{112,128},... | collective-permute-start | bytes 294920 | tf_op jit(solution)/shard_map/while/body/eval_jaxpr/ppermute | solution.py:16
  266.7 9.7 %collective-permute-start.1 = (f32[2,64,384]{2,1,0:T(8,128)S(1)}, f32[2,64,384]{2,1,0:T(8,128)S(1)}, u32[]{:S(2)}, u32[]{:S(2)}) collective-permute-start(f32[2,64,384]{2,1,0:T(8,128)S(1)} %maximum_add_fusion.2), channel_id=1, source_target_pairs={{0,16},{16,32},{32,48},{48,64},{64,80},{80,96},{96,112},{112,128},... | collective-permute-start | bytes 589832 | tf_op jit(solution)/shard_map/while/body/eval_jaxpr/ppermute | solution.py:16
  276.4 8.7 %collective-permute-start = (bf16[2,64,384]{2,1,0:T(8,128)(2,1)S(1)}, bf16[2,64,384]{2,1,0:T(8,128)(2,1)S(1)}, u32[]{:S(2)}, u32[]{:S(2)}) collective-permute-start(bf16[2,64,384]{2,1,0:T(8,128)(2,1)S(1)} %copy.171), channel_id=1, source_target_pairs={{0,16},{16,32},{32,48},{48,64},{64,80},{80,96},{96,112},{112,128},... | collective-permute-start | bytes 294920 | tf_op jit(solution)/shard_map/while/body/eval_jaxpr/ppermute | solution.py:16
  279.7 9.8 %collective-permute-start.1 = (f32[2,64,384]{2,1,0:T(8,128)S(1)}, f32[2,64,384]{2,1,0:T(8,128)S(1)}, u32[]{:S(2)}, u32[]{:S(2)}) collective-permute-start(f32[2,64,384]{2,1,0:T(8,128)S(1)} %maximum_add_fusion.2), channel_id=1, source_target_pairs={{0,16},{16,32},{32,48},{48,64},{64,80},{80,96},{96,112},{112,128},... | collective-permute-start | bytes 589832 | tf_op jit(solution)/shard_map/while/body/eval_jaxpr/ppermute | solution.py:16
  289.5 8.8 %collective-permute-start = (bf16[2,64,384]{2,1,0:T(8,128)(2,1)S(1)}, bf16[2,64,384]{2,1,0:T(8,128)(2,1)S(1)}, u32[]{:S(2)}, u32[]{:S(2)}) collective-permute-start(bf16[2,64,384]{2,1,0:T(8,128)(2,1)S(1)} %copy.171), channel_id=1, source_target_pairs={{0,16},{16,32},{32,48},{48,64},{64,80},{80,96},{96,112},{112,128},... | collective-permute-start | bytes 294920 | tf_op jit(solution)/shard_map/while/body/eval_jaxpr/ppermute | solution.py:16
  292.8 10.9 %collective-permute-start.1 = (f32[2,64,384]{2,1,0:T(8,128)S(1)}, f32[2,64,384]{2,1,0:T(8,128)S(1)}, u32[]{:S(2)}, u32[]{:S(2)}) collective-permute-start(f32[2,64,384]{2,1,0:T(8,128)S(1)} %maximum_add_fusion.2), channel_id=1, source_target_pairs={{0,16},{16,32},{32,48},{48,64},{64,80},{80,96},{96,112},{112,128},... | collective-permute-start | bytes 589832 | tf_op jit(solution)/shard_map/while/body/eval_jaxpr/ppermute | solution.py:16
  303.7 9.8 %collective-permute-start = (bf16[2,64,384]{2,1,0:T(8,128)(2,1)S(1)}, bf16[2,64,384]{2,1,0:T(8,128)(2,1)S(1)}, u32[]{:S(2)}, u32[]{:S(2)}) collective-permute-start(bf16[2,64,384]{2,1,0:T(8,128)(2,1)S(1)} %copy.171), channel_id=1, source_target_pairs={{0,16},{16,32},{32,48},{48,64},{64,80},{80,96},{96,112},{112,128},... | collective-permute-start | bytes 294920 | tf_op jit(solution)/shard_map/while/body/eval_jaxpr/ppermute | solution.py:16
  307.0 11.9 %collective-permute-start.1 = (f32[2,64,384]{2,1,0:T(8,128)S(1)}, f32[2,64,384]{2,1,0:T(8,128)S(1)}, u32[]{:S(2)}, u32[]{:S(2)}) collective-permute-start(f32[2,64,384]{2,1,0:T(8,128)S(1)} %maximum_add_fusion.2), channel_id=1, source_target_pairs={{0,16},{16,32},{32,48},{48,64},{64,80},{80,96},{96,112},{112,128},... | collective-permute-start | bytes 589832 | tf_op jit(solution)/shard_map/while/body/eval_jaxpr/ppermute | solution.py:16
  318.9 8.7 %collective-permute-start = (bf16[2,64,384]{2,1,0:T(8,128)(2,1)S(1)}, bf16[2,64,384]{2,1,0:T(8,128)(2,1)S(1)}, u32[]{:S(2)}, u32[]{:S(2)}) collective-permute-start(bf16[2,64,384]{2,1,0:T(8,128)(2,1)S(1)} %copy.171), channel_id=1, source_target_pairs={{0,16},{16,32},{32,48},{48,64},{64,80},{80,96},{96,112},{112,128},... | collective-permute-start | bytes 294920 | tf_op jit(solution)/shard_map/while/body/eval_jaxpr/ppermute | solution.py:16
  322.2 11.0 %collective-permute-start.1 = (f32[2,64,384]{2,1,0:T(8,128)S(1)}, f32[2,64,384]{2,1,0:T(8,128)S(1)}, u32[]{:S(2)}, u32[]{:S(2)}) collective-permute-start(f32[2,64,384]{2,1,0:T(8,128)S(1)} %maximum_add_fusion.2), channel_id=1, source_target_pairs={{0,16},{16,32},{32,48},{48,64},{64,80},{80,96},{96,112},{112,128},... | collective-permute-start | bytes 589832 | tf_op jit(solution)/shard_map/while/body/eval_jaxpr/ppermute | solution.py:16
  333.2 8.7 %collective-permute-start = (bf16[2,64,384]{2,1,0:T(8,128)(2,1)S(1)}, bf16[2,64,384]{2,1,0:T(8,128)(2,1)S(1)}, u32[]{:S(2)}, u32[]{:S(2)}) collective-permute-start(bf16[2,64,384]{2,1,0:T(8,128)(2,1)S(1)} %copy.171), channel_id=1, source_target_pairs={{0,16},{16,32},{32,48},{48,64},{64,80},{80,96},{96,112},{112,128},... | collective-permute-start | bytes 294920 | tf_op jit(solution)/shard_map/while/body/eval_jaxpr/ppermute | solution.py:16
  336.5 10.1 %collective-permute-start.1 = (f32[2,64,384]{2,1,0:T(8,128)S(1)}, f32[2,64,384]{2,1,0:T(8,128)S(1)}, u32[]{:S(2)}, u32[]{:S(2)}) collective-permute-start(f32[2,64,384]{2,1,0:T(8,128)S(1)} %maximum_add_fusion.2), channel_id=1, source_target_pairs={{0,16},{16,32},{32,48},{48,64},{64,80},{80,96},{96,112},{112,128},... | collective-permute-start | bytes 589832 | tf_op jit(solution)/shard_map/while/body/eval_jaxpr/ppermute | solution.py:16
  346.6 8.7 %collective-permute-start = (bf16[2,64,384]{2,1,0:T(8,128)(2,1)S(1)}, bf16[2,64,384]{2,1,0:T(8,128)(2,1)S(1)}, u32[]{:S(2)}, u32[]{:S(2)}) collective-permute-start(bf16[2,64,384]{2,1,0:T(8,128)(2,1)S(1)} %copy.171), channel_id=1, source_target_pairs={{0,16},{16,32},{32,48},{48,64},{64,80},{80,96},{96,112},{112,128},... | collective-permute-start | bytes 294920 | tf_op jit(solution)/shard_map/while/body/eval_jaxpr/ppermute | solution.py:16
  349.9 10.4 %collective-permute-start.1 = (f32[2,64,384]{2,1,0:T(8,128)S(1)}, f32[2,64,384]{2,1,0:T(8,128)S(1)}, u32[]{:S(2)}, u32[]{:S(2)}) collective-permute-start(f32[2,64,384]{2,1,0:T(8,128)S(1)} %maximum_add_fusion.2), channel_id=1, source_target_pairs={{0,16},{16,32},{32,48},{48,64},{64,80},{80,96},{96,112},{112,128},... | collective-permute-start | bytes 589832 | tf_op jit(solution)/shard_map/while/body/eval_jaxpr/ppermute | solution.py:16
  360.3 8.7 %collective-permute-start = (bf16[2,64,384]{2,1,0:T(8,128)(2,1)S(1)}, bf16[2,64,384]{2,1,0:T(8,128)(2,1)S(1)}, u32[]{:S(2)}, u32[]{:S(2)}) collective-permute-start(bf16[2,64,384]{2,1,0:T(8,128)(2,1)S(1)} %copy.171), channel_id=1, source_target_pairs={{0,16},{16,32},{32,48},{48,64},{64,80},{80,96},{96,112},{112,128},... | collective-permute-start | bytes 294920 | tf_op jit(solution)/shard_map/while/body/eval_jaxpr/ppermute | solution.py:16
  363.6 10.8 %collective-permute-start.1 = (f32[2,64,384]{2,1,0:T(8,128)S(1)}, f32[2,64,384]{2,1,0:T(8,128)S(1)}, u32[]{:S(2)}, u32[]{:S(2)}) collective-permute-start(f32[2,64,384]{2,1,0:T(8,128)S(1)} %maximum_add_fusion.2), channel_id=1, source_target_pairs={{0,16},{16,32},{32,48},{48,64},{64,80},{80,96},{96,112},{112,128},... | collective-permute-start | bytes 589832 | tf_op jit(solution)/shard_map/while/body/eval_jaxpr/ppermute | solution.py:16
  374.4 8.7 %collective-permute-start = (bf16[2,64,384]{2,1,0:T(8,128)(2,1)S(1)}, bf16[2,64,384]{2,1,0:T(8,128)(2,1)S(1)}, u32[]{:S(2)}, u32[]{:S(2)}) collective-permute-start(bf16[2,64,384]{2,1,0:T(8,128)(2,1)S(1)} %copy.171), channel_id=1, source_target_pairs={{0,16},{16,32},{32,48},{48,64},{64,80},{80,96},{96,112},{112,128},... | collective-permute-start | bytes 294920 | tf_op jit(solution)/shard_map/while/body/eval_jaxpr/ppermute | solution.py:16
  377.6 10.8 %collective-permute-start.1 = (f32[2,64,384]{2,1,0:T(8,128)S(1)}, f32[2,64,384]{2,1,0:T(8,128)S(1)}, u32[]{:S(2)}, u32[]{:S(2)}) collective-permute-start(f32[2,64,384]{2,1,0:T(8,128)S(1)} %maximum_add_fusion.2), channel_id=1, source_target_pairs={{0,16},{16,32},{32,48},{48,64},{64,80},{80,96},{96,112},{112,128},... | collective-permute-start | bytes 589832 | tf_op jit(solution)/shard_map/while/body/eval_jaxpr/ppermute | solution.py:16
  388.4 8.7 %collective-permute-start = (bf16[2,64,384]{2,1,0:T(8,128)(2,1)S(1)}, bf16[2,64,384]{2,1,0:T(8,128)(2,1)S(1)}, u32[]{:S(2)}, u32[]{:S(2)}) collective-permute-start(bf16[2,64,384]{2,1,0:T(8,128)(2,1)S(1)} %copy.171), channel_id=1, source_target_pairs={{0,16},{16,32},{32,48},{48,64},{64,80},{80,96},{96,112},{112,128},... | collective-permute-start | bytes 294920 | tf_op jit(solution)/shard_map/while/body/eval_jaxpr/ppermute | solution.py:16
  391.7 10.8 %collective-permute-start.1 = (f32[2,64,384]{2,1,0:T(8,128)S(1)}, f32[2,64,384]{2,1,0:T(8,128)S(1)}, u32[]{:S(2)}, u32[]{:S(2)}) collective-permute-start(f32[2,64,384]{2,1,0:T(8,128)S(1)} %maximum_add_fusion.2), channel_id=1, source_target_pairs={{0,16},{16,32},{32,48},{48,64},{64,80},{80,96},{96,112},{112,128},... | collective-permute-start | bytes 589832 | tf_op jit(solution)/shard_map/while/body/eval_jaxpr/ppermute | solution.py:16
  402.5 8.7 %collective-permute-start = (bf16[2,64,384]{2,1,0:T(8,128)(2,1)S(1)}, bf16[2,64,384]{2,1,0:T(8,128)(2,1)S(1)}, u32[]{:S(2)}, u32[]{:S(2)}) collective-permute-start(bf16[2,64,384]{2,1,0:T(8,128)(2,1)S(1)} %copy.171), channel_id=1, source_target_pairs={{0,16},{16,32},{32,48},{48,64},{64,80},{80,96},{96,112},{112,128},... | collective-permute-start | bytes 294920 | tf_op jit(solution)/shard_map/while/body/eval_jaxpr/ppermute | solution.py:16
  405.8 10.8 %collective-permute-start.1 = (f32[2,64,384]{2,1,0:T(8,128)S(1)}, f32[2,64,384]{2,1,0:T(8,128)S(1)}, u32[]{:S(2)}, u32[]{:S(2)}) collective-permute-start(f32[2,64,384]{2,1,0:T(8,128)S(1)} %maximum_add_fusion.2), channel_id=1, source_target_pairs={{0,16},{16,32},{32,48},{48,64},{64,80},{80,96},{96,112},{112,128},... | collective-permute-start | bytes 589832 | tf_op jit(solution)/shard_map/while/body/eval_jaxpr/ppermute | solution.py:16
  416.6 8.7 %collective-permute-start = (bf16[2,64,384]{2,1,0:T(8,128)(2,1)S(1)}, bf16[2,64,384]{2,1,0:T(8,128)(2,1)S(1)}, u32[]{:S(2)}, u32[]{:S(2)}) collective-permute-start(bf16[2,64,384]{2,1,0:T(8,128)(2,1)S(1)} %copy.171), channel_id=1, source_target_pairs={{0,16},{16,32},{32,48},{48,64},{64,80},{80,96},{96,112},{112,128},... | collective-permute-start | bytes 294920 | tf_op jit(solution)/shard_map/while/body/eval_jaxpr/ppermute | solution.py:16
  419.9 10.8 %collective-permute-start.1 = (f32[2,64,384]{2,1,0:T(8,128)S(1)}, f32[2,64,384]{2,1,0:T(8,128)S(1)}, u32[]{:S(2)}, u32[]{:S(2)}) collective-permute-start(f32[2,64,384]{2,1,0:T(8,128)S(1)} %maximum_add_fusion.2), channel_id=1, source_target_pairs={{0,16},{16,32},{32,48},{48,64},{64,80},{80,96},{96,112},{112,128},... | collective-permute-start | bytes 589832 | tf_op jit(solution)/shard_map/while/body/eval_jaxpr/ppermute | solution.py:16
  430.7 8.7 %collective-permute-start = (bf16[2,64,384]{2,1,0:T(8,128)(2,1)S(1)}, bf16[2,64,384]{2,1,0:T(8,128)(2,1)S(1)}, u32[]{:S(2)}, u32[]{:S(2)}) collective-permute-start(bf16[2,64,384]{2,1,0:T(8,128)(2,1)S(1)} %copy.171), channel_id=1, source_target_pairs={{0,16},{16,32},{32,48},{48,64},{64,80},{80,96},{96,112},{112,128},... | collective-permute-start | bytes 294920 | tf_op jit(solution)/shard_map/while/body/eval_jaxpr/ppermute | solution.py:16
  433.9 10.8 %collective-permute-start.1 = (f32[2,64,384]{2,1,0:T(8,128)S(1)}, f32[2,64,384]{2,1,0:T(8,128)S(1)}, u32[]{:S(2)}, u32[]{:S(2)}) collective-permute-start(f32[2,64,384]{2,1,0:T(8,128)S(1)} %maximum_add_fusion.2), channel_id=1, source_target_pairs={{0,16},{16,32},{32,48},{48,64},{64,80},{80,96},{96,112},{112,128},... | collective-permute-start | bytes 589832 | tf_op jit(solution)/shard_map/while/body/eval_jaxpr/ppermute | solution.py:16
  444.7 8.7 %collective-permute-start = (bf16[2,64,384]{2,1,0:T(8,128)(2,1)S(1)}, bf16[2,64,384]{2,1,0:T(8,128)(2,1)S(1)}, u32[]{:S(2)}, u32[]{:S(2)}) collective-permute-start(bf16[2,64,384]{2,1,0:T(8,128)(2,1)S(1)} %copy.171), channel_id=1, source_target_pairs={{0,16},{16,32},{32,48},{48,64},{64,80},{80,96},{96,112},{112,128},... | collective-permute-start | bytes 294920 | tf_op jit(solution)/shard_map/while/body/eval_jaxpr/ppermute | solution.py:16
  448.0 10.8 %collective-permute-start.1 = (f32[2,64,384]{2,1,0:T(8,128)S(1)}, f32[2,64,384]{2,1,0:T(8,128)S(1)}, u32[]{:S(2)}, u32[]{:S(2)}) collective-permute-start(f32[2,64,384]{2,1,0:T(8,128)S(1)} %maximum_add_fusion.2), channel_id=1, source_target_pairs={{0,16},{16,32},{32,48},{48,64},{64,80},{80,96},{96,112},{112,128},... | collective-permute-start | bytes 589832 | tf_op jit(solution)/shard_map/while/body/eval_jaxpr/ppermute | solution.py:16
  458.8 8.7 %collective-permute-start = (bf16[2,64,384]{2,1,0:T(8,128)(2,1)S(1)}, bf16[2,64,384]{2,1,0:T(8,128)(2,1)S(1)}, u32[]{:S(2)}, u32[]{:S(2)}) collective-permute-start(bf16[2,64,384]{2,1,0:T(8,128)(2,1)S(1)} %copy.171), channel_id=1, source_target_pairs={{0,16},{16,32},{32,48},{48,64},{64,80},{80,96},{96,112},{112,128},... | collective-permute-start | bytes 294920 | tf_op jit(solution)/shard_map/while/body/eval_jaxpr/ppermute | solution.py:16
  462.1 10.8 %collective-permute-start.1 = (f32[2,64,384]{2,1,0:T(8,128)S(1)}, f32[2,64,384]{2,1,0:T(8,128)S(1)}, u32[]{:S(2)}, u32[]{:S(2)}) collective-permute-start(f32[2,64,384]{2,1,0:T(8,128)S(1)} %maximum_add_fusion.2), channel_id=1, source_target_pairs={{0,16},{16,32},{32,48},{48,64},{64,80},{80,96},{96,112},{112,128},... | collective-permute-start | bytes 589832 | tf_op jit(solution)/shard_map/while/body/eval_jaxpr/ppermute | solution.py:16
  476.2 10.9 %collective-permute-start.1 = (f32[2,64,384]{2,1,0:T(8,128)S(1)}, f32[2,64,384]{2,1,0:T(8,128)S(1)}, u32[]{:S(2)}, u32[]{:S(2)}) collective-permute-start(f32[2,64,384]{2,1,0:T(8,128)S(1)} %maximum_add_fusion.2), channel_id=1, source_target_pairs={{0,16},{16,32},{32,48},{48,64},{64,80},{80,96},{96,112},{112,128},... | collective-permute-start | bytes 589832 | tf_op jit(solution)/shard_map/while/body/eval_jaxpr/ppermute | solution.py:16
  487.1 8.7 %collective-permute-start = (bf16[2,64,384]{2,1,0:T(8,128)(2,1)S(1)}, bf16[2,64,384]{2,1,0:T(8,128)(2,1)S(1)}, u32[]{:S(2)}, u32[]{:S(2)}) collective-permute-start(bf16[2,64,384]{2,1,0:T(8,128)(2,1)S(1)} %copy.171), channel_id=1, source_target_pairs={{0,16},{16,32},{32,48},{48,64},{64,80},{80,96},{96,112},{112,128},... | collective-permute-start | bytes 294920 | tf_op jit(solution)/shard_map/while/body/eval_jaxpr/ppermute | solution.py:16
  490.3 10.9 %collective-permute-start.1 = (f32[2,64,384]{2,1,0:T(8,128)S(1)}, f32[2,64,384]{2,1,0:T(8,128)S(1)}, u32[]{:S(2)}, u32[]{:S(2)}) collective-permute-start(f32[2,64,384]{2,1,0:T(8,128)S(1)} %maximum_add_fusion.2), channel_id=1, source_target_pairs={{0,16},{16,32},{32,48},{48,64},{64,80},{80,96},{96,112},{112,128},... | collective-permute-start | bytes 589832 | tf_op jit(solution)/shard_map/while/body/eval_jaxpr/ppermute | solution.py:16
  504.5 10.9 %collective-permute-start.1 = (f32[2,64,384]{2,1,0:T(8,128)S(1)}, f32[2,64,384]{2,1,0:T(8,128)S(1)}, u32[]{:S(2)}, u32[]{:S(2)}) collective-permute-start(f32[2,64,384]{2,1,0:T(8,128)S(1)} %maximum_add_fusion.2), channel_id=1, source_target_pairs={{0,16},{16,32},{32,48},{48,64},{64,80},{80,96},{96,112},{112,128},... | collective-permute-start | bytes 589832 | tf_op jit(solution)/shard_map/while/body/eval_jaxpr/ppermute | solution.py:16
  515.4 8.7 %collective-permute-start = (bf16[2,64,384]{2,1,0:T(8,128)(2,1)S(1)}, bf16[2,64,384]{2,1,0:T(8,128)(2,1)S(1)}, u32[]{:S(2)}, u32[]{:S(2)}) collective-permute-start(bf16[2,64,384]{2,1,0:T(8,128)(2,1)S(1)} %copy.171), channel_id=1, source_target_pairs={{0,16},{16,32},{32,48},{48,64},{64,80},{80,96},{96,112},{112,128},... | collective-permute-start | bytes 294920 | tf_op jit(solution)/shard_map/while/body/eval_jaxpr/ppermute | solution.py:16
  518.7 10.9 %collective-permute-start.1 = (f32[2,64,384]{2,1,0:T(8,128)S(1)}, f32[2,64,384]{2,1,0:T(8,128)S(1)}, u32[]{:S(2)}, u32[]{:S(2)}) collective-permute-start(f32[2,64,384]{2,1,0:T(8,128)S(1)} %maximum_add_fusion.2), channel_id=1, source_target_pairs={{0,16},{16,32},{32,48},{48,64},{64,80},{80,96},{96,112},{112,128},... | collective-permute-start | bytes 589832 | tf_op jit(solution)/shard_map/while/body/eval_jaxpr/ppermute | solution.py:16
  529.6 8.7 %collective-permute-start = (bf16[2,64,384]{2,1,0:T(8,128)(2,1)S(1)}, bf16[2,64,384]{2,1,0:T(8,128)(2,1)S(1)}, u32[]{:S(2)}, u32[]{:S(2)}) collective-permute-start(bf16[2,64,384]{2,1,0:T(8,128)(2,1)S(1)} %copy.171), channel_id=1, source_target_pairs={{0,16},{16,32},{32,48},{48,64},{64,80},{80,96},{96,112},{112,128},... | collective-permute-start | bytes 294920 | tf_op jit(solution)/shard_map/while/body/eval_jaxpr/ppermute | solution.py:16
  532.8 10.9 %collective-permute-start.1 = (f32[2,64,384]{2,1,0:T(8,128)S(1)}, f32[2,64,384]{2,1,0:T(8,128)S(1)}, u32[]{:S(2)}, u32[]{:S(2)}) collective-permute-start(f32[2,64,384]{2,1,0:T(8,128)S(1)} %maximum_add_fusion.2), channel_id=1, source_target_pairs={{0,16},{16,32},{32,48},{48,64},{64,80},{80,96},{96,112},{112,128},... | collective-permute-start | bytes 589832 | tf_op jit(solution)/shard_map/while/body/eval_jaxpr/ppermute | solution.py:16
  543.7 8.7 %collective-permute-start = (bf16[2,64,384]{2,1,0:T(8,128)(2,1)S(1)}, bf16[2,64,384]{2,1,0:T(8,128)(2,1)S(1)}, u32[]{:S(2)}, u32[]{:S(2)}) collective-permute-start(bf16[2,64,384]{2,1,0:T(8,128)(2,1)S(1)} %copy.171), channel_id=1, source_target_pairs={{0,16},{16,32},{32,48},{48,64},{64,80},{80,96},{96,112},{112,128},... | collective-permute-start | bytes 294920 | tf_op jit(solution)/shard_map/while/body/eval_jaxpr/ppermute | solution.py:16
  547.0 10.9 %collective-permute-start.1 = (f32[2,64,384]{2,1,0:T(8,128)S(1)}, f32[2,64,384]{2,1,0:T(8,128)S(1)}, u32[]{:S(2)}, u32[]{:S(2)}) collective-permute-start(f32[2,64,384]{2,1,0:T(8,128)S(1)} %maximum_add_fusion.2), channel_id=1, source_target_pairs={{0,16},{16,32},{32,48},{48,64},{64,80},{80,96},{96,112},{112,128},... | collective-permute-start | bytes 589832 | tf_op jit(solution)/shard_map/while/body/eval_jaxpr/ppermute | solution.py:16
  557.9 8.7 %collective-permute-start = (bf16[2,64,384]{2,1,0:T(8,128)(2,1)S(1)}, bf16[2,64,384]{2,1,0:T(8,128)(2,1)S(1)}, u32[]{:S(2)}, u32[]{:S(2)}) collective-permute-start(bf16[2,64,384]{2,1,0:T(8,128)(2,1)S(1)} %copy.171), channel_id=1, source_target_pairs={{0,16},{16,32},{32,48},{48,64},{64,80},{80,96},{96,112},{112,128},... | collective-permute-start | bytes 294920 | tf_op jit(solution)/shard_map/while/body/eval_jaxpr/ppermute | solution.py:16
  561.2 10.9 %collective-permute-start.1 = (f32[2,64,384]{2,1,0:T(8,128)S(1)}, f32[2,64,384]{2,1,0:T(8,128)S(1)}, u32[]{:S(2)}, u32[]{:S(2)}) collective-permute-start(f32[2,64,384]{2,1,0:T(8,128)S(1)} %maximum_add_fusion.2), channel_id=1, source_target_pairs={{0,16},{16,32},{32,48},{48,64},{64,80},{80,96},{96,112},{112,128},... | collective-permute-start | bytes 589832 | tf_op jit(solution)/shard_map/while/body/eval_jaxpr/ppermute | solution.py:16
  575.4 10.9 %collective-permute-start.1 = (f32[2,64,384]{2,1,0:T(8,128)S(1)}, f32[2,64,384]{2,1,0:T(8,128)S(1)}, u32[]{:S(2)}, u32[]{:S(2)}) collective-permute-start(f32[2,64,384]{2,1,0:T(8,128)S(1)} %maximum_add_fusion.2), channel_id=1, source_target_pairs={{0,16},{16,32},{32,48},{48,64},{64,80},{80,96},{96,112},{112,128},... | collective-permute-start | bytes 589832 | tf_op jit(solution)/shard_map/while/body/eval_jaxpr/ppermute | solution.py:16
  586.3 8.7 %collective-permute-start = (bf16[2,64,384]{2,1,0:T(8,128)(2,1)S(1)}, bf16[2,64,384]{2,1,0:T(8,128)(2,1)S(1)}, u32[]{:S(2)}, u32[]{:S(2)}) collective-permute-start(bf16[2,64,384]{2,1,0:T(8,128)(2,1)S(1)} %copy.171), channel_id=1, source_target_pairs={{0,16},{16,32},{32,48},{48,64},{64,80},{80,96},{96,112},{112,128},... | collective-permute-start | bytes 294920 | tf_op jit(solution)/shard_map/while/body/eval_jaxpr/ppermute | solution.py:16
  589.5 10.9 %collective-permute-start.1 = (f32[2,64,384]{2,1,0:T(8,128)S(1)}, f32[2,64,384]{2,1,0:T(8,128)S(1)}, u32[]{:S(2)}, u32[]{:S(2)}) collective-permute-start(f32[2,64,384]{2,1,0:T(8,128)S(1)} %maximum_add_fusion.2), channel_id=1, source_target_pairs={{0,16},{16,32},{32,48},{48,64},{64,80},{80,96},{96,112},{112,128},... | collective-permute-start | bytes 589832 | tf_op jit(solution)/shard_map/while/body/eval_jaxpr/ppermute | solution.py:16
  603.7 10.9 %collective-permute-start.1 = (f32[2,64,384]{2,1,0:T(8,128)S(1)}, f32[2,64,384]{2,1,0:T(8,128)S(1)}, u32[]{:S(2)}, u32[]{:S(2)}) collective-permute-start(f32[2,64,384]{2,1,0:T(8,128)S(1)} %maximum_add_fusion.2), channel_id=1, source_target_pairs={{0,16},{16,32},{32,48},{48,64},{64,80},{80,96},{96,112},{112,128},... | collective-permute-start | bytes 589832 | tf_op jit(solution)/shard_map/while/body/eval_jaxpr/ppermute | solution.py:16
  615.4 24.5 %all-to-all-start.3 = ((bf16[2,64,384]{2,0,1:T(2,128)(2,1)}), bf16[2,64,384]{2,0,1:T(2,128)(2,1)S(1)}, u32[]{:S(2)}, u32[]{:S(2)}) async-start(bf16[2,64,384]{2,0,1:T(2,128)(2,1)} %copy.116), calls=%async_computation.3 | async-start | bytes 196608 | tf_op jit(solution)/shard_map/all_to_all | solution.py:133
  639.9 11.0 %all-to-all-start.2 = ((bf16[4,128,384]{1,2,0:T(8,128)(2,1)}), bf16[4,128,384]{1,2,0:T(8,128)(2,1)S(1)}, u32[]{:S(2)}, u32[]{:S(2)}) async-start(bf16[4,128,384]{1,2,0:T(8,128)(2,1)} %copy.115), calls=%async_computation.2 | async-start | bytes 786432 | tf_op jit(solution)/shard_map/all_to_all | solution.py:132
  (16 other events, 625.1 us)
Sparse Core Ops, SparseCore 0:
  26.8 81.5 all-gather.1
where the time goes:
time: 662 us; the launch traced here: 659 us
  waiting for transfers between devices  342 us (52%)
  starting transfers between devices  154 us (23%)
  matrix products  64.3 us (10%)
  local copies, waits for them, and re-layouts  52.2 us (8%)
  other arithmetic  15 us (2%)
  between operations  14.3 us (2%)
  blocking collectives  12.6 us (2%)
    ppermute x64, waiting for transfers between devices, shifted(): lax.ppermute(array, axis, [(i, (i + by) % size) for i in range(size)])  264 us
    ppermute x64, starting transfers between devices, shifted(): lax.ppermute(array, axis, [(i, (i + by) % size) for i in range(size)])  124 us
    all_gather x1, waiting for transfers between devices, per_device(): piece = lax.all_gather(key_pair, 'blk', axis=1, tiled=True)  61.6 us
    all_to_all x1, starting transfers between devices, per_device(): lax.all_to_all(pair_grads, 'uly', split_axis=1, concat_axis=2, tiled=True)  21.1 us
    dynamic_slice x12, local copies, waits for them, and re-layouts, fold_keys(): result, unused = lax.scan(visit, running, (key_stack, value_stack))  19.1 us
  transfers between devices with their start and end apart: 68, of which 68 were waited for; matrix products, arithmetic and copies ran while one was open for 10% of the time, Pallas kernels for 0%

commit v1 on v0

v1 whole, which is shorter than its diff:
```python
import functools

import jax
import jax.numpy as jnp
from jax import lax
from jax.experimental import pallas as pl
from jax.experimental.pallas import tpu as pltpu
from jax.sharding import PartitionSpec as P

HEAD_DIM = 128
CELL = 8
SCALE = HEAD_DIM ** -0.5
LOG2E = 1.4426950408889634
F32 = jnp.float32
BF16 = jnp.bfloat16
ULY = 4


def dot_nn(a, b):
    return lax.dot_general(a, b, (((1,), (0,)), ((), ())), preferred_element_type=F32)


def dot_nt(a, b):
    return lax.dot_general(a, b, (((1,), (1,)), ((), ())), preferred_element_type=F32)


def dot_tn(a, b):
    return lax.dot_general(a, b, (((0,), (0,)), ((), ())), preferred_element_type=F32)


def kernel(
    nx, nz, heads, tok, rows,
    idx_ref, k_ref, v_ref, q_ref, g_ref,
    dq_out, dk_out, dv_out,
    kvsend, kv, qb, gb, e_buf, dp_buf, m_buf, stats, stats_in, fin,
    dq_acc, dqb, dqr, dqs, part, rbuf, ybuf, gkv_send, gkv,
    loc_sem, xkv_s, xkv_r, xq_s, xq_r, xg_s, xg_r, y_s, y_r,
    ring_s, ring_r, sib_s, sib_r, red_s, red_r, yr_s, yr_r, xo_s, xo_r, xd_s, xd_r,
):
    width = heads * HEAD_DIM
    half = nz // 2
    nq = 2 * nx * tok
    tq = min(256, nq)
    blk = lax.axis_index("blk")
    uly = lax.axis_index("uly")
    x = blk // nz
    z = blk % nz
    y = uly // 2
    c = uly % 2
    right = {"blk": x * nz + (z + 1) % nz}
    left = {"blk": x * nz + (z + nz - 1) % nz}
    ypeer = {"uly": (1 - y) * 2 + c}
    sib = {"uly": y * 2 + (1 - c)}

    def xpeer(j):
        return {"blk": ((x + j) % nx) * nz + z}

    def send(src, dst, s_sem, r_sem, dev):
        return pltpu.make_async_remote_copy(
            src_ref=src, dst_ref=dst, send_sem=s_sem, recv_sem=r_sem,
            device_id=dev, device_id_type=pl.DeviceIdType.MESH)

    barrier = pltpu.get_barrier_semaphore()
    others = [xpeer(j) for j in range(1, nx)] + [right, left, ypeer, sib]
    for dev in others:
        pl.semaphore_signal(barrier, inc=1, device_id=dev, device_id_type=pl.DeviceIdType.MESH)

    hot = (lax.broadcasted_iota(jnp.int32, (tok, rows), 0)
           == lax.rem(idx_ref[...], tok)).astype(F32).astype(BF16)
    for a, ref in enumerate((k_ref, v_ref)):
        for g in range(nx):
            for h in range(heads):
                col = (g * heads + h) * HEAD_DIM
                kvsend[g, h, a] = dot_tn(hot, ref[:, col:col + HEAD_DIM]).astype(BF16)

    pl.semaphore_wait(barrier, len(others))

    xrow = pl.ds(pl.multiple_of(x * rows, rows), rows)
    own_rows = pl.ds(pl.multiple_of((c * nx + x) * tok, tok), tok)
    own_cols = pl.ds(pl.multiple_of(x * width, width), width)
    kv_x = []
    for j in range(1, nx):
        g = (x + j) % nx
        kv_x.append(send(kvsend.at[g], kv.at[:, :, 0, y, xrow], xkv_s.at[j - 1], xkv_r.at[j - 1], xpeer(j)))
        kv_x[-1].start()
    q_x = []
    for j in range(1, nx):
        cols = pl.ds(pl.multiple_of(((x + j) % nx) * width, width), width)
        for src, dst, ss, rs in ((q_ref, qb, xq_s, xq_r), (g_ref, gb, xg_s, xg_r)):
            q_x.append(send(src.at[:, cols], dst.at[own_rows], ss.at[j - 1], rs.at[j - 1], xpeer(j)))
            q_x[-1].start()
    kv_own = pltpu.make_async_copy(kvsend.at[x], kv.at[:, :, 0, y, xrow], loc_sem.at[0])
    kv_own.start()
    q_own = pltpu.make_async_copy(q_ref.at[:, own_cols], qb.at[own_rows], loc_sem.at[1])
    q_own.start()
    g_own = pltpu.make_async_copy(g_ref.at[:, own_cols], gb.at[own_rows], loc_sem.at[2])
    g_own.start()

    stats[...] = jnp.zeros_like(stats)
    for h in range(heads):
        stats[h, 0:1] = jnp.full((1, nq), -1e30, F32)
    dq_acc[...] = jnp.zeros_like(dq_acc)

    kv_own.wait()
    for copy in kv_x:
        copy.wait_recv()
    kv_y = send(kv.at[:, :, 0, y], kv.at[:, :, 0, y], y_s, y_r, ypeer)
    kv_y.start()
    kv_y.wait_recv()

    def ring_full(s):
        last = 0 if isinstance(s, int) and s == 1 else 2 * (s - 1)
        src_a = last
        src_b = 0 if isinstance(s, int) and s == 1 else last + 1
        return (send(kv.at[:, :, src_a], kv.at[:, :, 2 * s], ring_s.at[0, s - 1], ring_r.at[0, s - 1], right),
                send(kv.at[:, :, src_b], kv.at[:, :, 2 * s + 1], ring_s.at[1, s - 1], ring_r.at[1, s - 1], left))

    def ring_half():
        last = 2 * (half - 1)
        return (send(kv.at[:, 0, last], kv.at[:, 0, 1], ring_s.at[0, half - 1], ring_r.at[0, half - 1], right),
                send(kv.at[:, 1, last + 1], kv.at[:, 1, 1], ring_s.at[1, half - 1], ring_r.at[1, half - 1], left))

    def forward(s):
        @pl.when(s < half - 1)
        def _():
            for copy in ring_full(s + 1):
                copy.start()

        @pl.when(s == half - 1)
        def _():
            for copy in ring_half():
                copy.start()

    for copy in ring_full(1):
        copy.start()

    q_own.wait()
    g_own.wait()
    for copy in q_x:
        copy.wait_recv()
    mine = pl.ds(pl.multiple_of(c * nx * tok, tok), nx * tok)
    share = [send(qb.at[mine], qb.at[mine], sib_s.at[0], sib_r.at[0], sib),
             send(gb.at[mine], gb.at[mine], sib_s.at[1], sib_r.at[1], sib)]
    for copy in share:
        copy.start()
    for copy in ring_full(1):
        copy.wait_recv()
    forward(jnp.int32(1))
    for copy in share:
        copy.wait_recv()

    def pass1(s):
        def head(h, carry):
            lanes = pl.ds(pl.multiple_of(h * HEAD_DIM, HEAD_DIM), HEAD_DIM)
            keys = kv[h, 0, pl.ds(2 * s, 2)].reshape(4 * nx * rows, HEAD_DIM)
            vals = kv[h, 1, pl.ds(2 * s, 2)].reshape(4 * nx * rows, HEAD_DIM)
            for t in range(nq // tq):
                ts = slice(t * tq, (t + 1) * tq)
                sc = dot_nt(keys, qb[ts, lanes]) * (SCALE * LOG2E)
                dp = dot_nt(vals, gb[ts, lanes])
                m_old = stats[h, 0:1, ts]
                m_new = jnp.maximum(m_old, jnp.max(sc, axis=0, keepdims=True))
                e = jnp.exp2(sc - m_new)
                a = jnp.exp2(m_old - m_new)
                e_buf[s, h, :, ts] = e
                dp_buf[s, h, :, ts] = dp
                m_buf[s, h, 0:1, ts] = m_new
                stats[h, 0:1, ts] = m_new
                stats[h, 1:2, ts] = stats[h, 1:2, ts] * a + jnp.sum(e, axis=0, keepdims=True)
                stats[h, 2:3, ts] = stats[h, 2:3, ts] * a + jnp.sum(e * dp, axis=0, keepdims=True)
            return carry
        lax.fori_loop(0, heads, head, 0)

    def gather_step(s, carry):
        pass1(s)

        @pl.when(s < half - 1)
        def _():
            for copy in ring_full(s + 1):
                copy.wait_recv()
            forward(s + 1)
        return carry

    lax.fori_loop(1, half, gather_step, 0)
    for copy in ring_half():
        copy.wait_recv()
    pass1(0)

    join = send(stats, stats_in, sib_s.at[2], sib_r.at[2], sib)
    join.start()
    join.wait()
    for h in range(heads):
        m1, m2 = stats[h, 0:1], stats_in[h, 0:1]
        m = jnp.maximum(m1, m2)
        a1, a2 = jnp.exp2(m1 - m), jnp.exp2(m2 - m)
        inv = 1.0 / (stats[h, 1:2] * a1 + stats_in[h, 1:2] * a2)
        fin[h, 0:1] = m
        fin[h, 1:2] = inv
        fin[h, 2:3] = (stats[h, 2:3] * a1 + stats_in[h, 2:3] * a2) * inv

    def pass2(s):
        def head(h, carry):
            lanes = pl.ds(pl.multiple_of(h * HEAD_DIM, HEAD_DIM), HEAD_DIM)
            keys = kv[h, 0, pl.ds(2 * s, 2)].reshape(4 * nx * rows, HEAD_DIM)
            dk = jnp.zeros((4 * nx * rows, HEAD_DIM), F32)
            dv = jnp.zeros((4 * nx * rows, HEAD_DIM), F32)
            for t in range(nq // tq):
                ts = slice(t * tq, (t + 1) * tq)
                r = jnp.exp2(m_buf[s, h, 0:1, ts] - fin[h, 0:1, ts]) * fin[h, 1:2, ts]
                p = e_buf[s, h, :, ts] * r
                ds = (p * (dp_buf[s, h, :, ts] - fin[h, 2:3, ts])).astype(BF16)
                dv = dv + dot_nn(p.astype(BF16), gb[ts, lanes])
                dk = dk + dot_nn(ds, qb[ts, lanes])
                dq_acc[h, :, ts] = dq_acc[h, :, ts] + dot_tn(keys, ds)
            part[h, 0, pl.ds(2 * s, 2)] = dk.astype(BF16).reshape(2, 2, nx * rows, HEAD_DIM)
            part[h, 1, pl.ds(2 * s, 2)] = dv.astype(BF16).reshape(2, 2, nx * rows, HEAD_DIM)
            return carry
        lax.fori_loop(0, heads, head, 0)

    def reduce_first():
        return (send(part.at[:, 0, 1], rbuf.at[0, 0, :, 0], red_s.at[0, 0], red_r.at[0, 0], right),
                send(part.at[:, 1, 1], rbuf.at[1, 0, :, 1], red_s.at[1, 0], red_r.at[1, 0], left))

    def reduce_full(t):
        d = half - t
        return (send(part.at[:, :, 2 * d + 1], rbuf.at[0, t], red_s.at[0, t], red_r.at[0, t], right),
                send(part.at[:, :, 2 * d], rbuf.at[1, t], red_s.at[1, t], red_r.at[1, t], left))

    def add_in(t, d, a):
        part[:, a, 2 * d + 1] = (part[:, a, 2 * d + 1].astype(F32) + rbuf[0, t, :, a].astype(F32)).astype(BF16)

    def add_in_left(t, d, a):
        part[:, a, 2 * d] = (part[:, a, 2 * d].astype(F32) + rbuf[1, t, :, a].astype(F32)).astype(BF16)

    def reduce_step(t, carry):
        d = half - t
        pass2(lax.rem(d, half))

        @pl.when(t == 0)
        def _():
            for copy in reduce_first():
                copy.start()

        @pl.when(t == 1)
        def _():
            for copy in reduce_first():
                copy.wait_recv()
            add_in(0, d, 0)
            add_in_left(0, d, 1)

        @pl.when(t > 1)
        def _():
            for copy in reduce_full(t - 1):
                copy.wait_recv()
            for a in range(2):
                add_in(t - 1, d, a)
                add_in_left(t - 1, d, a)

        @pl.when(t > 0)
        def _():
            for copy in reduce_full(t):
                copy.start()
        return carry

    lax.fori_loop(0, half, reduce_step, 0)

    for h in range(heads):
        for cc in range(2):
            for xs in range(nx):
                at = (cc * nx + xs) * tok
                dqb[cc, xs, :, h * HEAD_DIM:(h + 1) * HEAD_DIM] = (
                    jnp.transpose(dq_acc[h, :, at:at + tok]) * SCALE).astype(BF16)
    dq_sib = send(dqb.at[1 - c], dqr, sib_s.at[3], sib_r.at[3], sib)
    dq_sib.start()
    dq_sib.wait()
    for xs in range(nx):
        dqs[xs] = (dqb[c, xs].astype(F32) + dqr[xs].astype(F32)).astype(BF16)
    dq_x = []
    for j in range(1, nx):
        dq_x.append(send(dqs.at[(x + j) % nx], dq_out.at[:, own_cols], xd_s.at[j - 1], xd_r.at[j - 1], xpeer(j)))
        dq_x[-1].start()
    dq_own = pltpu.make_async_copy(dqs.at[x], dq_out.at[:, own_cols], loc_sem.at[3])
    dq_own.start()

    for copy in reduce_full(half - 1):
        copy.wait_recv()
    for h in range(heads):
        for a in range(2):
            total = (part[h, a, 0].astype(F32) + rbuf[0, half - 1, h, a].astype(F32)
                     + rbuf[1, half - 1, h, a].astype(F32))
            part[h, a, 0] = total.astype(BF16)
    yr = send(part.at[:, :, 0, 1 - y], ybuf, yr_s, yr_r, ypeer)
    yr.start()
    yr.wait()
    for h in range(heads):
        for a in range(2):
            total = part[h, a, 0, y].astype(F32) + ybuf[h, a].astype(F32)
            if a == 0:
                total = total * SCALE
            total = total.astype(BF16)
            for xs in range(nx):
                gkv_send[xs, h, a] = total[xs * rows:(xs + 1) * rows]
    out_x = []
    for j in range(1, nx):
        out_x.append(send(gkv_send.at[(x + j) % nx], gkv.at[x], xo_s.at[j - 1], xo_r.at[j - 1], xpeer(j)))
        out_x[-1].start()
    out_own = pltpu.make_async_copy(gkv_send.at[x], gkv.at[x], loc_sem.at[4])
    out_own.start()
    out_own.wait()
    for copy in out_x:
        copy.wait_recv()
    for a, ref in enumerate((dk_out, dv_out)):
        for g in range(nx):
            for h in range(heads):
                col = (g * heads + h) * HEAD_DIM
                ref[:, col:col + HEAD_DIM] = dot_nn(hot, gkv[g, h, a]).astype(BF16)

    for copy in kv_x + q_x + [kv_y] + share:
        copy.wait_send()
    dq_own.wait()
    for copy in dq_x:
        copy.wait()
    for copy in out_x:
        copy.wait_send()

    def drain(s, carry):
        for copy in ring_full(s):
            copy.wait_send()
        for copy in reduce_full(s):
            copy.wait_send()
        return carry

    lax.fori_loop(1, half, drain, 0)
    for copy in ring_half() + reduce_first():
        copy.wait_send()


def per_device(nx, nz, queries, key_input, value_input, grad_out, keep_index):
    tok, columns = queries.shape
    rows = keep_index.shape[0]
    heads = columns // HEAD_DIM // nx
    width = heads * HEAD_DIM
    half = nz // 2
    nq = 2 * nx * tok
    nk = 4 * nx * rows
    slab = (nx * rows, HEAD_DIM)
    dma = pltpu.SemaphoreType.DMA
    vmem = pltpu.VMEM
    out = jax.ShapeDtypeStruct((tok, columns), BF16)
    in_vmem = pl.BlockSpec(memory_space=pltpu.VMEM)
    in_any = pl.BlockSpec(memory_space=pl.ANY)
    flops = 2 * 6 * heads * nq * (half * nk) * HEAD_DIM
    return pl.pallas_call(
        functools.partial(kernel, nx, nz, heads, tok, rows),
        out_shape=(out, out, out),
        in_specs=[in_vmem, in_vmem, in_vmem, in_any, in_any],
        out_specs=(in_vmem, in_vmem, in_vmem),
        scratch_shapes=[
            vmem((nx, heads, 2, rows, HEAD_DIM), BF16),
            vmem((heads, 2, nz, 2) + slab, BF16),
            vmem((nq, width), BF16),
            vmem((nq, width), BF16),
            vmem((half, heads, nk, nq), F32),
            vmem((half, heads, nk, nq), F32),
            vmem((half, heads, 8, nq), F32),
            vmem((heads, 8, nq), F32),
            vmem((heads, 8, nq), F32),
            vmem((heads, 8, nq), F32),
            vmem((heads, HEAD_DIM, nq), F32),
            vmem((2, nx, tok, width), BF16),
            vmem((nx, tok, width), BF16),
            vmem((nx, tok, width), BF16),
            vmem((heads, 2, nz, 2) + slab, BF16),
            vmem((2, half, heads, 2, 2) + slab, BF16),
            vmem((heads, 2) + slab, BF16),
            vmem((nx, heads, 2, rows, HEAD_DIM), BF16),
            vmem((nx, heads, 2, rows, HEAD_DIM), BF16),
            dma((5,)),
            dma((nx - 1,)), dma((nx - 1,)),
            dma((nx - 1,)), dma((nx - 1,)),
            dma((nx - 1,)), dma((nx - 1,)),
            dma, dma,
            dma((2, half)), dma((2, half)),
            dma((4,)), dma((4,)),
            dma((2, half)), dma((2, half)),
            dma, dma,
            dma((nx - 1,)), dma((nx - 1,)),
            dma((nx - 1,)), dma((nx - 1,)),
        ],
        compiler_params=pltpu.CompilerParams(
            collective_id=0, has_side_effects=True, vmem_limit_bytes=56 * 2 ** 20),
        cost_estimate=pl.CostEstimate(
            flops=flops, bytes_accessed=7 * tok * columns * 2, transcendentals=heads * nq * half * nk),
    )(keep_index.reshape(1, rows), key_input, value_input, queries, grad_out)


def build(mesh, nx, nz):
    rows_spec = P(("rep", "blk", "uly"), None)
    return jax.shard_map(
        functools.partial(per_device, nx, nz), mesh=mesh,
        in_specs=(rows_spec,) * 4 + (P(("rep", "blk", "uly")),),
        out_specs=(rows_spec,) * 3, check_vma=False)


def solution(mesh):
    return build(mesh, 4, 8)
```

time: 662 us -> 86.2 us (0.13)
  the two profiles are of different devices: /device:TPU:1 before, /device:TPU:40 now
where the time goes in v1:
time: 86.2 us; the launch traced here: 86 us
  Pallas kernels  81.6 us (95%)
  local copies, waits for them, and re-layouts  3.7 us (4%)
    pallas_call x1, Pallas kernels, per_device(): pl.pallas_call(functools.partial(kernel, nx, nz, heads, tok, rows), out_s...  81.6 us
    unnamed x7, local copies, waits for them, and re-layouts  3.7 us

profile of v1, /device:TPU:40, one launch (start us, length us, event | category | flops | bytes accessed | tf_op | source)
XLA Modules:
  0.0 86.0 jit_solution(2508889877594272310)
XLA Ops:
  0.6 81.6 %shard_map.76 = (bf16[128,1536]{1,0:T(8,128)(2,1)}, bf16[128,1536]{1,0:T(8,128)(2,1)}, bf16[128,1536]{1,0:T(8,128)(2,1)}) custom-call(s32[1,16]{1,0:T(1,128)} %bitcast.1, bf16[128,1536]{1,0:T(8,128)(2,1)} %k_ref.1, bf16[128,1536]{1,0:T(8,128)(2,1)} %v_ref.1, bf16[128,1536]{1,0:T(8,128)(2,1)} %q_ref.1, bf16[128,1536]{1,0:T(8,128)(2,1)} %g_ref.1), custom_call_target="tpu_custom_call" | custom-call | flops 4831838208 | bytes 2752512 | tf_op jit(solution)/shard_map/pallas_call | solution.py:353
  82.3 0.0 copy-start.1
  82.3 1.8 %copy.11 = bf16[128,1536]{1,0:T(8,128)(2,1)} copy(bf16[128,1536]{1,0:T(8,128)(2,1)} %get-tuple-element.6) | data formatting | bytes 786432
  84.1 0.0 copy-done.1
  84.1 0.0 copy-start
  84.1 0.7 copy.12
  84.8 0.4 copy-done
  85.2 0.7 copy.13
Async XLA Ops:
  82.3 1.8 %copy-start.1 = (bf16[128,1536]{1,0:T(8,128)(2,1)S(1)}, bf16[128,1536]{1,0:T(8,128)(2,1)}, u32[]{:S(2)}) copy-start(bf16[128,1536]{1,0:T(8,128)(2,1)} %get-tuple-element.7) | copy-start | bytes 1179652
  84.1 1.1 %copy-start = (bf16[128,1536]{1,0:T(8,128)(2,1)S(1)}, bf16[128,1536]{1,0:T(8,128)(2,1)}, u32[]{:S(2)}) copy-start(bf16[128,1536]{1,0:T(8,128)(2,1)} %get-tuple-element.8) | copy-start | bytes 1179652

commit v2 on v1

v2 whole, which is shorter than its diff:
```python
import functools

import jax
import jax.numpy as jnp
from jax import lax
from jax.experimental import pallas as pl
from jax.experimental.pallas import tpu as pltpu
from jax.sharding import PartitionSpec as P

HEAD_DIM = 128
CELL = 8
SCALE = HEAD_DIM ** -0.5
LOG2E = 1.4426950408889634
F32 = jnp.float32
BF16 = jnp.bfloat16
ULY = 4


def dot_nn(a, b):
    return lax.dot_general(a, b, (((1,), (0,)), ((), ())), preferred_element_type=F32)


def dot_nt(a, b):
    return lax.dot_general(a, b, (((1,), (1,)), ((), ())), preferred_element_type=F32)


def dot_tn(a, b):
    return lax.dot_general(a, b, (((0,), (0,)), ((), ())), preferred_element_type=F32)


def one_hot(idx_ref, tok, rows):
    return (lax.broadcasted_iota(jnp.int32, (tok, rows), 0)
            == lax.rem(idx_ref[...], tok)).astype(F32).astype(BF16)


def kernel(
    nx, nz, heads, tok, rows,
    idx_ref, k_ref, v_ref, q_ref, g_ref,
    dq_out, gkv,
    kvsend, kv, qb, gb, e_buf, dp_buf, m_buf, stats, stats_in, fin,
    dq_acc, dqb, dqr, dqs, part, rs_buf, rr_buf, ys_buf, yr_buf, gkv_send,
    loc_sem, xkv_s, xkv_r, xq_s, xq_r, xg_s, xg_r, y_s, y_r,
    ring_s, ring_r, sib_s, sib_r, join_s, join_r, red_s, red_r, yr_s, yr_r, xo_s, xo_r, xd_s, xd_r,
):
    width = heads * HEAD_DIM
    half = nz // 2
    hq = nx * tok
    nq = 2 * hq
    nk = 4 * nx * rows
    tq = min(256, hq)
    blk = lax.axis_index("blk")
    uly = lax.axis_index("uly")
    x = blk // nz
    z = blk % nz
    y = uly // 2
    c = uly % 2
    right = {"blk": x * nz + (z + 1) % nz}
    left = {"blk": x * nz + (z + nz - 1) % nz}
    ypeer = {"uly": (1 - y) * 2 + c}
    sib = {"uly": y * 2 + (1 - c)}
    hop = [1, nx - 1] + list(range(2, nx - 1)) if nx > 2 else [1]

    def xpeer(j):
        return {"blk": ((x + j) % nx) * nz + z}

    def send(src, dst, s_sem, r_sem, dev):
        return pltpu.make_async_remote_copy(
            src_ref=src, dst_ref=dst, send_sem=s_sem, recv_sem=r_sem,
            device_id=dev, device_id_type=pl.DeviceIdType.MESH)

    def start(copies):
        for copy in copies:
            copy.start()

    def received(copies):
        for copy in copies:
            copy.wait_recv()

    def sent(copies):
        for copy in copies:
            copy.wait_send()

    barrier = pltpu.get_barrier_semaphore()
    others = [xpeer(j) for j in hop] + [right, left, ypeer, sib]
    for dev in others:
        pl.semaphore_signal(barrier, inc=1, device_id=dev, device_id_type=pl.DeviceIdType.MESH)

    hot = one_hot(idx_ref, tok, rows)
    for a, ref in enumerate((k_ref, v_ref)):
        for g in range(nx):
            for h in range(heads):
                col = (g * heads + h) * HEAD_DIM
                kvsend[g, h, a] = dot_tn(hot, ref[:, col:col + HEAD_DIM]).astype(BF16)

    pl.semaphore_wait(barrier, len(others))

    xrow = pl.ds(pl.multiple_of(x * rows, rows), rows)

    def token_rows(j):
        return pl.ds(pl.multiple_of((c * nx + (x + nx - j) % nx) * tok, tok), tok)

    def group_cols(j):
        return pl.ds(pl.multiple_of(((x + j) % nx) * width, width), width)

    kv_x = [send(kvsend.at[(x + j) % nx], kv.at[:, :, 0, y, xrow], xkv_s.at[j - 1], xkv_r.at[j - 1], xpeer(j))
            for j in hop]
    start(kv_x)
    kv_own = pltpu.make_async_copy(kvsend.at[x], kv.at[:, :, 0, y, xrow], loc_sem.at[0])
    kv_own.start()
    q_x = {j: [send(q_ref.at[:, group_cols(j)], qb.at[token_rows(0)], xq_s.at[j - 1], xq_r.at[j - 1], xpeer(j)),
               send(g_ref.at[:, group_cols(j)], gb.at[token_rows(0)], xg_s.at[j - 1], xg_r.at[j - 1], xpeer(j))]
           for j in hop}
    for j in hop:
        start(q_x[j])
    q_own = [pltpu.make_async_copy(q_ref.at[:, group_cols(0)], qb.at[token_rows(0)], loc_sem.at[1]),
             pltpu.make_async_copy(g_ref.at[:, group_cols(0)], gb.at[token_rows(0)], loc_sem.at[2])]
    start(q_own)

    share = {0: [send(q_ref.at[:, group_cols(0)], qb.at[token_rows(0)], sib_s.at[0, 0], sib_r.at[0, 0], sib),
                 send(g_ref.at[:, group_cols(0)], gb.at[token_rows(0)], sib_s.at[1, 0], sib_r.at[1, 0], sib)]}
    for j in hop:
        share[j] = [send(qb.at[token_rows(j)], qb.at[token_rows(j)], sib_s.at[0, j], sib_r.at[0, j], sib),
                    send(gb.at[token_rows(j)], gb.at[token_rows(j)], sib_s.at[1, j], sib_r.at[1, j], sib)]
    start(share[0])

    stats[...] = jnp.zeros_like(stats)
    for h in range(heads):
        stats[h, 0:1] = jnp.full((1, nq), -1e30, F32)
    dq_acc[...] = jnp.zeros_like(dq_acc)

    def ring(kind, s):
        def cut(slot, a):
            if kind == 0:
                return kv.at[1:heads, a, slot, y]
            return kv.at[0, a, slot]
        a_src, b_src = (0, 0) if s == 1 else (2 * s - 2, 2 * s - 1)
        if s < half:
            ways = ((a_src, 2 * s, slice(None)), (b_src, 2 * s + 1, slice(None)))
        else:
            ways = ((a_src, 1, 0), (b_src, 1, 1))
        return [send(cut(src, a), cut(dst, a), ring_s.at[kind, w, s - 1], ring_r.at[kind, w, s - 1], dev)
                for w, ((src, dst, a), dev) in enumerate(zip(ways, (right, left)))]

    def over_y(slot):
        return send(kv.at[1:heads, :, slot, y], kv.at[1:heads, :, slot, y], y_s.at[slot], y_r.at[slot], ypeer)

    def handle(s):
        slots = (2 * s, 2 * s + 1) if s < half else (1,)
        for kind in range(2):
            received(ring(kind, s))
            if s < half:
                start(ring(kind, s + 1))
            if kind == 0:
                start([over_y(slot) for slot in slots])

    kv_own.wait()
    received(kv_x)
    start(ring(0, 1))
    y_first = send(kv.at[0, :, 0, y], kv.at[0, :, 0, y], y_s.at[nz], y_r.at[nz], ypeer)
    start([y_first, over_y(0)])
    received([y_first])
    start(ring(1, 1))
    for copy in q_own:
        copy.wait()
    early = min(2, half)
    handle(1)
    for j in hop:
        received(q_x[j])
        start(share[j])
    for s in range(2, early + 1):
        handle(s)

    def pass1(s, qh, h):
        lanes = pl.ds(pl.multiple_of(h * HEAD_DIM, HEAD_DIM), HEAD_DIM)
        keys = kv[h, 0, pl.ds(2 * s, 2)].reshape(nk, HEAD_DIM)
        vals = kv[h, 1, pl.ds(2 * s, 2)].reshape(nk, HEAD_DIM)
        for t in range(hq // tq):
            ts = pl.ds(pl.multiple_of(qh * hq + t * tq, tq), tq)
            sc = dot_nt(keys, qb[ts, lanes]) * (SCALE * LOG2E)
            dp = dot_nt(vals, gb[ts, lanes])
            m_old = stats[h, 0:1, ts]
            m_new = jnp.maximum(m_old, jnp.max(sc, axis=0, keepdims=True))
            e = jnp.exp2(sc - m_new)
            a = jnp.exp2(m_old - m_new)
            e_buf[s, h, :, ts] = e
            dp_buf[s, h, :, ts] = dp
            m_buf[s, h, 0:1, ts] = m_new
            stats[h, 0:1, ts] = m_new
            stats[h, 1:2, ts] = stats[h, 1:2, ts] * a + jnp.sum(e, axis=0, keepdims=True)
            stats[h, 2:3, ts] = stats[h, 2:3, ts] * a + jnp.sum(e * dp, axis=0, keepdims=True)

    def gather_step(i, carry):
        n = i // 2
        s = n + 1
        later = lax.rem(i, 2)
        for m in range(half - 1):
            @pl.when(i == 2 * m)
            def _():
                if m >= 1 and m + 2 <= half:
                    handle(m + 2)
                received([over_y(2 * m + 2), over_y(2 * m + 3)])

        @pl.when(i == 1)
        def _():
            for j in [0] + hop:
                received(share[j])

        def head(h, inner):
            pass1(s, lax.rem(c + later, 2), h)
            return inner
        lax.fori_loop(0, heads, head, 0)
        return carry

    lax.fori_loop(0, 2 * (half - 1), gather_step, 0)
    received([over_y(0), over_y(1)])

    def join(h):
        return send(stats.at[h], stats_in.at[h], join_s.at[h], join_r.at[h], sib)

    def last_head(h, carry):
        def both(qh, inner):
            pass1(0, qh, h)
            return inner
        lax.fori_loop(0, 2, both, 0)
        join(h).start()
        return carry

    lax.fori_loop(0, heads, last_head, 0)

    def finish_stats(h):
        join(h).wait_recv()
        m1, m2 = stats[h, 0:1], stats_in[h, 0:1]
        m = jnp.maximum(m1, m2)
        a1, a2 = jnp.exp2(m1 - m), jnp.exp2(m2 - m)
        inv = 1.0 / (stats[h, 1:2] * a1 + stats_in[h, 1:2] * a2)
        fin[h, 0:1] = m
        fin[h, 1:2] = inv
        fin[h, 2:3] = (stats[h, 2:3] * a1 + stats_in[h, 2:3] * a2) * inv

    def pass2(s, h):
        lanes = pl.ds(pl.multiple_of(h * HEAD_DIM, HEAD_DIM), HEAD_DIM)
        keys = kv[h, 0, pl.ds(2 * s, 2)].reshape(nk, HEAD_DIM)
        dk = jnp.zeros((nk, HEAD_DIM), F32)
        dv = jnp.zeros((nk, HEAD_DIM), F32)
        for t in range(nq // tq):
            ts = slice(t * tq, (t + 1) * tq)
            r = jnp.exp2(m_buf[s, h, 0:1, ts] - fin[h, 0:1, ts]) * fin[h, 1:2, ts]
            p = e_buf[s, h, :, ts] * r
            ds = (p * (dp_buf[s, h, :, ts] - fin[h, 2:3, ts])).astype(BF16)
            dv = dv + dot_nn(p.astype(BF16), gb[ts, lanes])
            dk = dk + dot_nn(ds, qb[ts, lanes])
            dq_acc[h, :, ts] = dq_acc[h, :, ts] + dot_tn(keys, ds)
        part[h, 0, pl.ds(2 * s, 2)] = dk.astype(BF16).reshape(2, 2, nx * rows, HEAD_DIM)
        part[h, 1, pl.ds(2 * s, 2)] = dv.astype(BF16).reshape(2, 2, nx * rows, HEAD_DIM)

    def mine(kind, slot, a):
        return part.at[1:heads, a, slot, y] if kind == 0 else part.at[0, a, slot]

    def box(kind, w, t, a):
        return rs_buf.at[w, t, :, a] if kind == 0 else rr_buf.at[w, t, a]

    def reduce_half(kind):
        return [send(mine(kind, 1, w), box(kind, w, 0, w), red_s.at[kind, w, 0], red_r.at[kind, w, 0], dev)
                for w, dev in enumerate((right, left))]

    def reduce_full(kind, t):
        d = half - t
        return [send(mine(kind, 2 * d + 1 - w, slice(None)), box(kind, w, t, slice(None)),
                     red_s.at[kind, w, t], red_r.at[kind, w, t], dev)
                for w, dev in enumerate((right, left))]

    def reduce_y(slot):
        return send(part.at[1:heads, :, slot, 1 - y], ys_buf.at[slot], yr_s.at[slot], yr_r.at[slot], ypeer)

    def add_y(slot):
        reduce_y(slot).wait_recv()
        part[1:heads, :, slot, y] = (part[1:heads, :, slot, y].astype(F32) + ys_buf[slot].astype(F32)).astype(BF16)

    def add_box(kind, w, t, slot, a):
        if kind == 0:
            part[1:heads, a, slot, y] = (
                part[1:heads, a, slot, y].astype(F32) + rs_buf[w, t, :, a].astype(F32)).astype(BF16)
        else:
            part[0, a, slot] = (part[0, a, slot].astype(F32) + rr_buf[w, t, a].astype(F32)).astype(BF16)

    def produce(t):
        s = lax.rem(half - t, half)

        def head(h, carry):
            @pl.when(t == 0)
            def _():
                finish_stats(h)
            pass2(s, h)

            @pl.when((t == 0) & (h == 0))
            def _():
                start(reduce_half(1))
            return carry
        lax.fori_loop(0, heads, head, 0)

        @pl.when(t == 0)
        def _():
            start([reduce_y(1), reduce_y(0)])

        @pl.when(t > 0)
        def _():
            start([reduce_y(2 * s + 1), reduce_y(2 * s)])

    def pass_on(t):
        d = half - t

        @pl.when(t == 0)
        def _():
            add_y(1)
            start(reduce_half(0))

        @pl.when(t > 0)
        def _():
            for kind in (1, 0):
                if kind == 0:
                    add_y(2 * d + 1)
                    add_y(2 * d)

                @pl.when(t == 1)
                def _():
                    received(reduce_half(kind))
                    for w in range(2):
                        add_box(kind, w, 0, 2 * d + 1 - w, w)

                @pl.when(t > 1)
                def _():
                    received(reduce_full(kind, t - 1))
                    for w in range(2):
                        for a in range(2):
                            add_box(kind, w, t - 1, 2 * d + 1 - w, a)
                start(reduce_full(kind, t))

    dq_sib = send(dqb.at[1 - c], dqr, sib_s.at[0, nx], sib_r.at[0, nx], sib)

    def reduce_step(t, carry):
        @pl.when(t < half)
        def _():
            produce(t)

        @pl.when(t == half)
        def _():
            for h in range(heads):
                for cc in range(2):
                    for xs in range(nx):
                        at = (cc * nx + xs) * tok
                        dqb[cc, xs, :, h * HEAD_DIM:(h + 1) * HEAD_DIM] = (
                            jnp.transpose(dq_acc[h, :, at:at + tok]) * SCALE).astype(BF16)
            dq_sib.start()

        @pl.when(t > 0)
        def _():
            pass_on(t - 1)
        return carry

    lax.fori_loop(0, half + 1, reduce_step, 0)

    dq_sib.wait()
    for xs in range(nx):
        dqs[xs] = (dqb[c, xs].astype(F32) + dqr[xs].astype(F32)).astype(BF16)
    dq_x = [send(dqs.at[(x + j) % nx], dq_out.at[:, group_cols(0)], xd_s.at[j - 1], xd_r.at[j - 1], xpeer(j))
            for j in hop]
    start(dq_x)
    dq_own = pltpu.make_async_copy(dqs.at[x], dq_out.at[:, group_cols(0)], loc_sem.at[3])
    dq_own.start()

    received(reduce_full(1, half - 1))
    part[0, :, 0] = (part[0, :, 0].astype(F32) + rr_buf[0, half - 1].astype(F32)
                     + rr_buf[1, half - 1].astype(F32)).astype(BF16)
    y_last = send(part.at[0, :, 0, 1 - y], yr_buf, yr_s.at[nz], yr_r.at[nz], ypeer)
    y_last.start()

    def put(h, a, total):
        if a == 0:
            total = total * SCALE
        total = total.astype(BF16)
        for xs in range(nx):
            gkv_send[xs, h, a] = total[xs * rows:(xs + 1) * rows]

    reduce_y(0).wait_recv()
    received(reduce_full(0, half - 1))
    for h in range(1, heads):
        for a in range(2):
            put(h, a, part[h, a, 0, y].astype(F32) + ys_buf[0, h - 1, a].astype(F32)
                + rs_buf[0, half - 1, h - 1, a].astype(F32) + rs_buf[1, half - 1, h - 1, a].astype(F32))
    y_last.wait_recv()
    for a in range(2):
        put(0, a, part[0, a, 0, y].astype(F32) + yr_buf[a].astype(F32))
    out_x = [send(gkv_send.at[(x + j) % nx], gkv.at[x], xo_s.at[j - 1], xo_r.at[j - 1], xpeer(j)) for j in hop]
    start(out_x)
    out_own = pltpu.make_async_copy(gkv_send.at[x], gkv.at[x], loc_sem.at[4])
    out_own.start()

    sent(kv_x)
    for j in hop:
        sent(q_x[j])
    for j in [0] + hop:
        sent(share[j])
    for kind in range(2):
        for s in range(1, half + 1):
            sent(ring(kind, s))
        sent(reduce_half(kind))
        for t in range(1, half):
            sent(reduce_full(kind, t))
    for slot in range(nz):
        sent([over_y(slot), reduce_y(slot)])
    sent([y_first, y_last])
    for h in range(heads):
        join(h).wait_send()
    dq_own.wait()
    for copy in dq_x:
        copy.wait()
    out_own.wait()
    for copy in out_x:
        copy.wait()


def place(nx, heads, tok, rows, idx_ref, dq_ref, gkv_ref, dq_out, dk_out, dv_out):
    dq_out[...] = dq_ref[...]
    hot = one_hot(idx_ref, tok, rows)
    for a, ref in enumerate((dk_out, dv_out)):
        for g in range(nx):
            for h in range(heads):
                col = (g * heads + h) * HEAD_DIM
                ref[:, col:col + HEAD_DIM] = dot_nn(hot, gkv_ref[g, h, a]).astype(BF16)


def per_device(nx, nz, queries, key_input, value_input, grad_out, keep_index):
    tok, columns = queries.shape
    rows = keep_index.shape[0]
    heads = columns // HEAD_DIM // nx
    width = heads * HEAD_DIM
    half = nz // 2
    nq = 2 * nx * tok
    nk = 4 * nx * rows
    slab = (nx * rows, HEAD_DIM)
    dma = pltpu.SemaphoreType.DMA
    vmem = pltpu.VMEM
    out = jax.ShapeDtypeStruct((tok, columns), BF16)
    compact = (nx, heads, 2, rows, HEAD_DIM)
    in_vmem = pl.BlockSpec(memory_space=pltpu.VMEM)
    in_any = pl.BlockSpec(memory_space=pl.ANY)
    flops = 2 * 6 * heads * nq * (half * nk) * HEAD_DIM
    index = keep_index.reshape(1, rows)
    dq, gkv = pl.pallas_call(
        functools.partial(kernel, nx, nz, heads, tok, rows),
        out_shape=(out, jax.ShapeDtypeStruct(compact, BF16)),
        in_specs=[in_vmem, in_vmem, in_vmem, in_any, in_any],
        out_specs=(in_vmem, in_vmem),
        scratch_shapes=[
            vmem(compact, BF16),
            vmem((heads, 2, nz, 2) + slab, BF16),
            vmem((nq, width), BF16),
            vmem((nq, width), BF16),
            vmem((half, heads, nk, nq), F32),
            vmem((half, heads, nk, nq), F32),
            vmem((half, heads, 8, nq), F32),
            vmem((heads, 8, nq), F32),
            vmem((heads, 8, nq), F32),
            vmem((heads, 8, nq), F32),
            vmem((heads, HEAD_DIM, nq), F32),
            vmem((2, nx, tok, width), BF16),
            vmem((nx, tok, width), BF16),
            vmem((nx, tok, width), BF16),
            vmem((heads, 2, nz, 2) + slab, BF16),
            vmem((2, half, heads - 1, 2) + slab, BF16),
            vmem((2, half, 2, 2) + slab, BF16),
            vmem((nz, heads - 1, 2) + slab, BF16),
            vmem((2,) + slab, BF16),
            vmem(compact, BF16),
            dma((5,)),
            dma((nx - 1,)), dma((nx - 1,)),
            dma((nx - 1,)), dma((nx - 1,)),
            dma((nx - 1,)), dma((nx - 1,)),
            dma((nz + 1,)), dma((nz + 1,)),
            dma((2, 2, half)), dma((2, 2, half)),
            dma((2, nx + 1)), dma((2, nx + 1)),
            dma((heads,)), dma((heads,)),
            dma((2, 2, half)), dma((2, 2, half)),
            dma((nz + 1,)), dma((nz + 1,)),
            dma((nx - 1,)), dma((nx - 1,)),
            dma((nx - 1,)), dma((nx - 1,)),
        ],
        compiler_params=pltpu.CompilerParams(
            collective_id=0, has_side_effects=True, vmem_limit_bytes=56 * 2 ** 20),
        cost_estimate=pl.CostEstimate(
            flops=flops, bytes_accessed=7 * tok * columns * 2, transcendentals=heads * nq * half * nk),
    )(index, key_input, value_input, queries, grad_out)
    return pl.pallas_call(
        functools.partial(place, nx, heads, tok, rows),
        out_shape=(out, out, out),
        in_specs=[in_vmem] * 3,
        out_specs=(in_vmem,) * 3,
    )(index, dq, gkv)


def build(mesh, nx, nz):
    rows_spec = P(("rep", "blk", "uly"), None)
    return jax.shard_map(
        functools.partial(per_device, nx, nz), mesh=mesh,
        in_specs=(rows_spec,) * 4 + (P(("rep", "blk", "uly")),),
        out_specs=(rows_spec,) * 3, check_vma=False)


def solution(mesh):
    return build(mesh, 4, 8)
```

time: 86.2 us -> 72.4 us (0.84)
  Pallas kernels: 81.6 us -> 71.6 us
  local copies, waits for them, and re-layouts: 3.7 us -> 0 us
    pallas_call x1, Pallas kernels: 81.6 us -> 69.4 us  [per_device(): pl.pallas_call(functools.partial(kernel, nx, nz, heads, tok, rows), out_s...]
    unnamed x7 -> x0, local copies, waits for them, and re-layouts: 3.7 us -> none
    pallas_call x0 -> x1, Pallas kernels: none -> 2.27 us  [per_device(): pl.pallas_call(functools.partial(place, nx, heads, tok, rows), out_shape=...]
where the time goes in v2:
time: 72.4 us; the launch traced here: 72.3 us
  Pallas kernels  71.6 us (99%)
    pallas_call x1, Pallas kernels, per_device(): pl.pallas_call(functools.partial(kernel, nx, nz, heads, tok, rows), out_s...  69.4 us
    pallas_call x1, Pallas kernels, per_device(): pl.pallas_call(functools.partial(place, nx, heads, tok, rows), out_shape=...  2.27 us

profile of v2, /device:TPU:40, one launch (start us, length us, event | category | flops | bytes accessed | tf_op | source)
XLA Modules:
  0.0 72.3 jit_solution(18091908830932201466)
XLA Ops:
  0.6 69.4 %shard_map.76 = (bf16[128,1536]{1,0:T(8,128)(2,1)}, bf16[4,3,2,16,128]{4,3,2,1,0:T(8,128)(2,1)}) custom-call(s32[1,16]{1,0:T(1,128)} %bitcast.1, bf16[128,1536]{1,0:T(8,128)(2,1)} %k_ref.1, bf16[128,1536]{1,0:T(8,128)(2,1)} %v_ref.1, bf16[128,1536]{1,0:T(8,128)(2,1)} %q_ref.1, bf16[128,1536]{1,0:T(8,128)(2,1)} %g_ref.1), custom_call_target="tpu_custom_call" | custom-call | flops 4831838208 | bytes 2752512 | tf_op jit(solution)/shard_map/pallas_call | solution.py:449
  70.0 2.3 %shard_map.77 = (bf16[128,1536]{1,0:T(8,128)(2,1)}, bf16[128,1536]{1,0:T(8,128)(2,1)}, bf16[128,1536]{1,0:T(8,128)(2,1)}) custom-call(s32[1,16]{1,0:T(1,128)} %bitcast.2, bf16[128,1536]{1,0:T(8,128)(2,1)} %get-tuple-element.5.dq_ref, bf16[4,3,2,16,128]{4,3,2,1,0:T(8,128)(2,1)} %get-tuple-element.6.gkv_ref), custom_call_target="tpu_custom_call" | custom-call | tf_op jit(solution)/shard_map/pallas_call | solution.py:493

commit v3 on v2

--- a/solution.py
+++ b/solution.py
@@ -54,8 +54,10 @@
     z = blk % nz
     y = uly // 2
     c = uly % 2
-    right = {"blk": x * nz + (z + 1) % nz}
-    left = {"blk": x * nz + (z + nz - 1) % nz}
+
+    def along(by):
+        return {"blk": x * nz + (z + nz + by) % nz}
+
     ypeer = {"uly": (1 - y) * 2 + c}
     sib = {"uly": y * 2 + (1 - c)}
     hop = [1, nx - 1] + list(range(2, nx - 1)) if nx > 2 else [1]
@@ -81,7 +83,7 @@
             copy.wait_send()
 
     barrier = pltpu.get_barrier_semaphore()
-    others = [xpeer(j) for j in hop] + [right, left, ypeer, sib]
+    others = [xpeer(j) for j in hop] + [along(1), along(-1), along(2), along(-2), ypeer, sib]
     for dev in others:
         pl.semaphore_signal(barrier, inc=1, device_id=dev, device_id_type=pl.DeviceIdType.MESH)
 
@@ -133,13 +135,13 @@
             if kind == 0:
                 return kv.at[1:heads, a, slot, y]
             return kv.at[0, a, slot]
-        a_src, b_src = (0, 0) if s == 1 else (2 * s - 2, 2 * s - 1)
+        a_src, b_src, by = ((0, 0, s), (4, 5, s - 2))[s > 2]
         if s < half:
             ways = ((a_src, 2 * s, slice(None)), (b_src, 2 * s + 1, slice(None)))
         else:
             ways = ((a_src, 1, 0), (b_src, 1, 1))
-        return [send(cut(src, a), cut(dst, a), ring_s.at[kind, w, s - 1], ring_r.at[kind, w, s - 1], dev)
-                for w, ((src, dst, a), dev) in enumerate(zip(ways, (right, left)))]
+        return [send(cut(src, a), cut(dst, a), ring_s.at[kind, w, s - 1], ring_r.at[kind, w, s - 1], along(way))
+                for w, ((src, dst, a), way) in enumerate(zip(ways, (by, -by)))]
 
     def over_y(slot):
         return send(kv.at[1:heads, :, slot, y], kv.at[1:heads, :, slot, y], y_s.at[slot], y_r.at[slot], ypeer)
@@ -148,27 +150,26 @@
         slots = (2 * s, 2 * s + 1) if s < half else (1,)
         for kind in range(2):
             received(ring(kind, s))
-            if s < half:
-                start(ring(kind, s + 1))
+            if s == 2 and half == 4:
+                start(ring(kind, 3) + ring(kind, 4))
             if kind == 0:
                 start([over_y(slot) for slot in slots])
 
     kv_own.wait()
     received(kv_x)
-    start(ring(0, 1))
+    start(ring(0, 2) + ring(0, 1))
     y_first = send(kv.at[0, :, 0, y], kv.at[0, :, 0, y], y_s.at[nz], y_r.at[nz], ypeer)
     start([y_first, over_y(0)])
     received([y_first])
-    start(ring(1, 1))
+    start(ring(1, 2) + ring(1, 1))
     for copy in q_own:
         copy.wait()
-    early = min(2, half)
+    if half > 2:
+        handle(2)
     handle(1)
     for j in hop:
         received(q_x[j])
         start(share[j])
-    for s in range(2, early + 1):
-        handle(s)
 
     def pass1(s, qh, h):
         lanes = pl.ds(pl.multiple_of(h * HEAD_DIM, HEAD_DIM), HEAD_DIM)
@@ -196,7 +197,7 @@
         for m in range(half - 1):
             @pl.when(i == 2 * m)
             def _():
-                if m >= 1 and m + 2 <= half:
+                if m >= 1:
                     handle(m + 2)
                 received([over_y(2 * m + 2), over_y(2 * m + 3)])
 
@@ -212,12 +213,17 @@
         return carry
 
     lax.fori_loop(0, 2 * (half - 1), gather_step, 0)
-    received([over_y(0), over_y(1)])
+    if half == 2:
+        handle(2)
 
     def join(h):
         return send(stats.at[h], stats_in.at[h], join_s.at[h], join_r.at[h], sib)
 
     def last_head(h, carry):
+        @pl.when(h == 1)
+        def _():
+            received([over_y(0), over_y(1)])
+
         def both(qh, inner):
             pass1(0, qh, h)
             return inner
@@ -256,18 +262,19 @@
     def mine(kind, slot, a):
         return part.at[1:heads, a, slot, y] if kind == 0 else part.at[0, a, slot]
 
-    def box(kind, w, t, a):
-        return rs_buf.at[w, t, :, a] if kind == 0 else rr_buf.at[w, t, a]
-
-    def reduce_half(kind):
-        return [send(mine(kind, 1, w), box(kind, w, 0, w), red_s.at[kind, w, 0], red_r.at[kind, w, 0], dev)
-                for w, dev in enumerate((right, left))]
-
-    def reduce_full(kind, t):
-        d = half - t
-        return [send(mine(kind, 2 * d + 1 - w, slice(None)), box(kind, w, t, slice(None)),
-                     red_s.at[kind, w, t], red_r.at[kind, w, t], dev)
-                for w, dev in enumerate((right, left))]
+    def box(kind, w, n, a):
+        return rs_buf.at[w, n, :, a] if kind == 0 else rr_buf.at[w, n, a]
+
+    def reduce(kind, n):
+        ways = []
+        for w, sign in enumerate((1, -1)):
+            if n == half:
+                slot, a, by = 1, w, 2
+            else:
+                slot, a, by = 2 * n + 1 - w, slice(None), (n if n < 3 else 1)
+            ways.append(send(mine(kind, slot, a), box(kind, w, n - 1, a),
+                             red_s.at[kind, w, n - 1], red_r.at[kind, w, n - 1], along(sign * by)))
+        return ways
 
     def reduce_y(slot):
         return send(part.at[1:heads, :, slot, 1 - y], ys_buf.at[slot], yr_s.at[slot], yr_r.at[slot], ypeer)
@@ -276,64 +283,64 @@
         reduce_y(slot).wait_recv()
         part[1:heads, :, slot, y] = (part[1:heads, :, slot, y].astype(F32) + ys_buf[slot].astype(F32)).astype(BF16)
 
-    def add_box(kind, w, t, slot, a):
-        if kind == 0:
-            part[1:heads, a, slot, y] = (
-                part[1:heads, a, slot, y].astype(F32) + rs_buf[w, t, :, a].astype(F32)).astype(BF16)
-        else:
-            part[0, a, slot] = (part[0, a, slot].astype(F32) + rr_buf[w, t, a].astype(F32)).astype(BF16)
+    def add_boxes(kind):
+        received(reduce(kind, 3) + reduce(kind, 4))
+        for w in range(2):
+            slot = 5 - w
+            for a in range(2):
+                if kind == 0:
+                    total = part[1:heads, a, slot, y].astype(F32) + rs_buf[w, 2, :, a].astype(F32)
+                    if a == w:
+                        total = total + rs_buf[w, 3, :, a].astype(F32)
+                    part[1:heads, a, slot, y] = total.astype(BF16)
+                else:
+                    total = part[0, a, slot].astype(F32) + rr_buf[w, 2, a].astype(F32)
+                    if a == w:
+                        total = total + rr_buf[w, 3, a].astype(F32)
+                    part[0, a, slot] = total.astype(BF16)
+
+    order = [3, 4, 1, 2] if half == 4 else [2, 1]
+
+    def pair_of(t):
+        return lax.rem(t + 3, 4) if half == 4 else t
 
     def produce(t):
-        s = lax.rem(half - t, half)
-
-        def head(h, carry):
+        s = pair_of(t)
+
+        def head(n, carry):
+            h = lax.rem(n + 1, heads)
+
             @pl.when(t == 0)
             def _():
                 finish_stats(h)
             pass2(s, h)
 
-            @pl.when((t == 0) & (h == 0))
+            @pl.when(n == heads - 2)
             def _():
-                start(reduce_half(1))
+                for k, place in enumerate(order):
+                    @pl.when(t == k)
+                    def _():
+                        start([reduce_y(slot) for slot in ((2 * place + 1, 2 * place) if place < half else (1,))])
             return carry
         lax.fori_loop(0, heads, head, 0)
-
-        @pl.when(t == 0)
-        def _():
-            start([reduce_y(1), reduce_y(0)])
-
-        @pl.when(t > 0)
-        def _():
-            start([reduce_y(2 * s + 1), reduce_y(2 * s)])
+        for k, place in enumerate(order):
+            if place != 2 or half == 2:
+                @pl.when(t == k)
+                def _():
+                    start(reduce(1, place))
 
     def pass_on(t):
-        d = half - t
-
-        @pl.when(t == 0)
-        def _():
-            add_y(1)
-            start(reduce_half(0))
-
-        @pl.when(t > 0)
-        def _():
-            for kind in (1, 0):
-                if kind == 0:
-                    add_y(2 * d + 1)
-                    add_y(2 * d)
-
-                @pl.when(t == 1)
-                def _():
-                    received(reduce_half(kind))
-                    for w in range(2):
-                        add_box(kind, w, 0, 2 * d + 1 - w, w)
-
-                @pl.when(t > 1)
-                def _():
-                    received(reduce_full(kind, t - 1))
-                    for w in range(2):
-                        for a in range(2):
-                            add_box(kind, w, t - 1, 2 * d + 1 - w, a)
-                start(reduce_full(kind, t))
+        for k, place in enumerate(order):
+            @pl.when(t == k)
+            def _():
+                for slot in ((2 * place + 1, 2 * place) if place < half else (1,)):
+                    add_y(slot)
+                if place == 2 and half == 4:
+                    for kind in (1, 0):
+                        add_boxes(kind)
+                        start(reduce(kind, 2))
+                else:
+                    start(reduce(0, place))
 
     dq_sib = send(dqb.at[1 - c], dqr, sib_s.at[0, nx], sib_r.at[0, nx], sib)
 
@@ -344,6 +351,7 @@
 
         @pl.when(t == half)
         def _():
+            start([reduce_y(0)])
             for h in range(heads):
                 for cc in range(2):
                     for xs in range(nx):
@@ -368,9 +376,26 @@
     dq_own = pltpu.make_async_copy(dqs.at[x], dq_out.at[:, group_cols(0)], loc_sem.at[3])
     dq_own.start()
 
-    received(reduce_full(1, half - 1))
-    part[0, :, 0] = (part[0, :, 0].astype(F32) + rr_buf[0, half - 1].astype(F32)
-                     + rr_buf[1, half - 1].astype(F32)).astype(BF16)
+    received(reduce(1, 1) + reduce(1, 2))
+
+    def total_r(a):
+        total = part[0, a, 0].astype(F32)
+        for w in range(2):
+            total = total + rr_buf[w, 0, a].astype(F32)
+            if half == 4 or a == w:
+                total = total + rr_buf[w, 1, a].astype(F32)
+        return total
+
+    def total_s(h, a):
+        total = part[h, a, 0, y].astype(F32) + ys_buf[0, h - 1, a].astype(F32)
+        for w in range(2):
+            total = total + rs_buf[w, 0, h - 1, a].astype(F32)
+            if half == 4 or a == w:
+                total = total + rs_buf[w, 1, h - 1, a].astype(F32)
+        return total
+
+    for a in range(2):
+        part[0, a, 0] = total_r(a).astype(BF16)
     y_last = send(part.at[0, :, 0, 1 - y], yr_buf, yr_s.at[nz], yr_r.at[nz], ypeer)
     y_last.start()
 
@@ -382,11 +407,10 @@
             gkv_send[xs, h, a] = total[xs * rows:(xs + 1) * rows]
 
     reduce_y(0).wait_recv()
-    received(reduce_full(0, half - 1))
+    received(reduce(0, 1) + reduce(0, 2))
     for h in range(1, heads):
         for a in range(2):
-            put(h, a, part[h, a, 0, y].astype(F32) + ys_buf[0, h - 1, a].astype(F32)
-                + rs_buf[0, half - 1, h - 1, a].astype(F32) + rs_buf[1, half - 1, h - 1, a].astype(F32))
+            put(h, a, total_s(h, a))
     y_last.wait_recv()
     for a in range(2):
         put(0, a, part[0, a, 0, y].astype(F32) + yr_buf[a].astype(F32))
@@ -402,10 +426,7 @@
         sent(share[j])
     for kind in range(2):
         for s in range(1, half + 1):
-            sent(ring(kind, s))
-        sent(reduce_half(kind))
-        for t in range(1, half):
-            sent(reduce_full(kind, t))
+            sent(ring(kind, s) + reduce(kind, s))
     for slot in range(nz):
         sent([over_y(slot), reduce_y(slot)])
     sent([y_first, y_last])

time: 72.4 us -> 74.9 us (1.035)
  the two profiles are of different devices: /device:TPU:40 before, /device:TPU:4 now
where the time goes in v3:
time: 74.9 us; the launch traced here: 74.7 us
  Pallas kernels  74.1 us (99%)
    pallas_call x1, Pallas kernels, per_device(): pl.pallas_call(functools.partial(kernel, nx, nz, heads, tok, rows), out_s...  71.8 us
    pallas_call x1, Pallas kernels, per_device(): pl.pallas_call(functools.partial(place, nx, heads, tok, rows), out_shape=...  2.27 us

profile of v3, /device:TPU:4, one launch (start us, length us, event | category | flops | bytes accessed | tf_op | source)
XLA Modules:
  0.0 74.7 jit_solution(15081352785759296064)
XLA Ops:
  0.6 71.8 %shard_map.76 = (bf16[128,1536]{1,0:T(8,128)(2,1)}, bf16[4,3,2,16,128]{4,3,2,1,0:T(8,128)(2,1)}) custom-call(s32[1,16]{1,0:T(1,128)} %bitcast.1, bf16[128,1536]{1,0:T(8,128)(2,1)} %k_ref.1, bf16[128,1536]{1,0:T(8,128)(2,1)} %v_ref.1, bf16[128,1536]{1,0:T(8,128)(2,1)} %q_ref.1, bf16[128,1536]{1,0:T(8,128)(2,1)} %g_ref.1), custom_call_target="tpu_custom_call" | custom-call | flops 4831838208 | bytes 2752512 | tf_op jit(solution)/shard_map/pallas_call | solution.py:470
  72.5 2.3 %shard_map.77 = (bf16[128,1536]{1,0:T(8,128)(2,1)}, bf16[128,1536]{1,0:T(8,128)(2,1)}, bf16[128,1536]{1,0:T(8,128)(2,1)}) custom-call(s32[1,16]{1,0:T(1,128)} %bitcast.2, bf16[128,1536]{1,0:T(8,128)(2,1)} %get-tuple-element.5.dq_ref, bf16[4,3,2,16,128]{4,3,2,1,0:T(8,128)(2,1)} %get-tuple-element.6.gkv_ref), custom_call_target="tpu_custom_call" | custom-call | tf_op jit(solution)/shard_map/pallas_call | solution.py:514

commit v4 on v3

--- a/solution.py
+++ b/solution.py
@@ -135,7 +135,7 @@
             if kind == 0:
                 return kv.at[1:heads, a, slot, y]
             return kv.at[0, a, slot]
-        a_src, b_src, by = ((0, 0, s), (4, 5, s - 2))[s > 2]
+        a_src, b_src, by = ((0, 0, 1), (2, 3, 1), (4, 5, 1), (4, 5, 2))[s - 1]
         if s < half:
             ways = ((a_src, 2 * s, slice(None)), (b_src, 2 * s + 1, slice(None)))
         else:
@@ -147,29 +147,30 @@
         return send(kv.at[1:heads, :, slot, y], kv.at[1:heads, :, slot, y], y_s.at[slot], y_r.at[slot], ypeer)
 
     def handle(s):
-        slots = (2 * s, 2 * s + 1) if s < half else (1,)
         for kind in range(2):
-            received(ring(kind, s))
-            if s == 2 and half == 4:
-                start(ring(kind, 3) + ring(kind, 4))
-            if kind == 0:
-                start([over_y(slot) for slot in slots])
+            onward = [ring(kind, n) for n in ((2,), (3, 4), (), ())[s - 1]]
+            for w, copy in enumerate(ring(kind, s)):
+                copy.wait_recv()
+                start([copies[w] for copies in onward])
+                if kind == 0 and s < half:
+                    over_y(2 * s + w).start()
+            if kind == 0 and s == half:
+                over_y(1).start()
 
     kv_own.wait()
     received(kv_x)
-    start(ring(0, 2) + ring(0, 1))
+    start(ring(0, 1))
     y_first = send(kv.at[0, :, 0, y], kv.at[0, :, 0, y], y_s.at[nz], y_r.at[nz], ypeer)
     start([y_first, over_y(0)])
     received([y_first])
-    start(ring(1, 2) + ring(1, 1))
+    start(ring(1, 1))
     for copy in q_own:
         copy.wait()
-    if half > 2:
-        handle(2)
     handle(1)
     for j in hop:
         received(q_x[j])
         start(share[j])
+    handle(2)
 
     def pass1(s, qh, h):
         lanes = pl.ds(pl.multiple_of(h * HEAD_DIM, HEAD_DIM), HEAD_DIM)
@@ -213,9 +214,6 @@
         return carry
 
     lax.fori_loop(0, 2 * (half - 1), gather_step, 0)
-    if half == 2:
-        handle(2)
-
     def join(h):
         return send(stats.at[h], stats_in.at[h], join_s.at[h], join_r.at[h], sib)
 
@@ -271,7 +269,7 @@
             if n == half:
                 slot, a, by = 1, w, 2
             else:
-                slot, a, by = 2 * n + 1 - w, slice(None), (n if n < 3 else 1)
+                slot, a, by = 2 * n + 1 - w, slice(None), 1
             ways.append(send(mine(kind, slot, a), box(kind, w, n - 1, a),
                              red_s.at[kind, w, n - 1], red_r.at[kind, w, n - 1], along(sign * by)))
         return ways
@@ -283,29 +281,30 @@
         reduce_y(slot).wait_recv()
         part[1:heads, :, slot, y] = (part[1:heads, :, slot, y].astype(F32) + ys_buf[slot].astype(F32)).astype(BF16)
 
-    def add_boxes(kind):
-        received(reduce(kind, 3) + reduce(kind, 4))
+    def relay(kind, n):
         for w in range(2):
-            slot = 5 - w
+            slot = 2 * n + 1 - w
+            if kind == 0:
+                add_y(slot)
+            received([reduce(kind, n + 1)[w]] + ([reduce(kind, 4)[w]] if n == 2 else []))
             for a in range(2):
+                far = n == 2 and a == w
                 if kind == 0:
-                    total = part[1:heads, a, slot, y].astype(F32) + rs_buf[w, 2, :, a].astype(F32)
-                    if a == w:
+                    total = part[1:heads, a, slot, y].astype(F32) + rs_buf[w, n, :, a].astype(F32)
+                    if far:
                         total = total + rs_buf[w, 3, :, a].astype(F32)
                     part[1:heads, a, slot, y] = total.astype(BF16)
                 else:
-                    total = part[0, a, slot].astype(F32) + rr_buf[w, 2, a].astype(F32)
-                    if a == w:
+                    total = part[0, a, slot].astype(F32) + rr_buf[w, n, a].astype(F32)
+                    if far:
                         total = total + rr_buf[w, 3, a].astype(F32)
                     part[0, a, slot] = total.astype(BF16)
-
-    order = [3, 4, 1, 2] if half == 4 else [2, 1]
-
-    def pair_of(t):
-        return lax.rem(t + 3, 4) if half == 4 else t
+            reduce(kind, n)[w].start()
+
+    order = [4, 3, 2, 1]
 
     def produce(t):
-        s = pair_of(t)
+        s = lax.rem(half - t, half)
 
         def head(n, carry):
             h = lax.rem(n + 1, heads)
@@ -324,7 +323,7 @@
             return carry
         lax.fori_loop(0, heads, head, 0)
         for k, place in enumerate(order):
-            if place != 2 or half == 2:
+            if place > 2:
                 @pl.when(t == k)
                 def _():
                     start(reduce(1, place))
@@ -333,14 +332,16 @@
         for k, place in enumerate(order):
             @pl.when(t == k)
             def _():
-                for slot in ((2 * place + 1, 2 * place) if place < half else (1,)):
-                    add_y(slot)
-                if place == 2 and half == 4:
-                    for kind in (1, 0):
-                        add_boxes(kind)
-                        start(reduce(kind, 2))
+                if place < 3:
+                    relay(1, place)
+                    relay(0, place)
+                elif place == 3:
+                    for w in range(2):
+                        add_y(7 - w)
+                        reduce(0, 3)[w].start()
                 else:
-                    start(reduce(0, place))
+                    add_y(1)
+                    start(reduce(0, 4))
 
     dq_sib = send(dqb.at[1 - c], dqr, sib_s.at[0, nx], sib_r.at[0, nx], sib)
 
@@ -376,22 +377,18 @@
     dq_own = pltpu.make_async_copy(dqs.at[x], dq_out.at[:, group_cols(0)], loc_sem.at[3])
     dq_own.start()
 
-    received(reduce(1, 1) + reduce(1, 2))
+    received(reduce(1, 1))
 
     def total_r(a):
         total = part[0, a, 0].astype(F32)
         for w in range(2):
             total = total + rr_buf[w, 0, a].astype(F32)
-            if half == 4 or a == w:
-                total = total + rr_buf[w, 1, a].astype(F32)
         return total
 
     def total_s(h, a):
         total = part[h, a, 0, y].astype(F32) + ys_buf[0, h - 1, a].astype(F32)
         for w in range(2):
             total = total + rs_buf[w, 0, h - 1, a].astype(F32)
-            if half == 4 or a == w:
-                total = total + rs_buf[w, 1, h - 1, a].astype(F32)
         return total
 
     for a in range(2):
@@ -407,7 +404,7 @@
             gkv_send[xs, h, a] = total[xs * rows:(xs + 1) * rows]
 
     reduce_y(0).wait_recv()
-    received(reduce(0, 1) + reduce(0, 2))
+    received(reduce(0, 1))
     for h in range(1, heads):
         for a in range(2):
             put(h, a, total_s(h, a))

time: 74.9 us -> 69.8 us (0.932)
  the two profiles are of different devices: /device:TPU:4 before, /device:TPU:16 now
where the time goes in v4:
time: 69.8 us; the launch traced here: 69.6 us
  Pallas kernels  69 us (99%)
    pallas_call x1, Pallas kernels, per_device(): pl.pallas_call(functools.partial(kernel, nx, nz, heads, tok, rows), out_s...  66.7 us
    pallas_call x1, Pallas kernels, per_device(): pl.pallas_call(functools.partial(place, nx, heads, tok, rows), out_shape=...  2.28 us

profile of v4, /device:TPU:16, one launch (start us, length us, event | category | flops | bytes accessed | tf_op | source)
XLA Modules:
  0.0 69.6 jit_solution(5220667494736456009)
XLA Ops:
  0.6 66.7 %shard_map.76 = (bf16[128,1536]{1,0:T(8,128)(2,1)}, bf16[4,3,2,16,128]{4,3,2,1,0:T(8,128)(2,1)}) custom-call(s32[1,16]{1,0:T(1,128)} %bitcast.1, bf16[128,1536]{1,0:T(8,128)(2,1)} %k_ref.1, bf16[128,1536]{1,0:T(8,128)(2,1)} %v_ref.1, bf16[128,1536]{1,0:T(8,128)(2,1)} %q_ref.1, bf16[128,1536]{1,0:T(8,128)(2,1)} %g_ref.1), custom_call_target="tpu_custom_call" | custom-call | flops 4831838208 | bytes 2752512 | tf_op jit(solution)/shard_map/pallas_call | solution.py:467
  67.3 2.3 %shard_map.77 = (bf16[128,1536]{1,0:T(8,128)(2,1)}, bf16[128,1536]{1,0:T(8,128)(2,1)}, bf16[128,1536]{1,0:T(8,128)(2,1)}) custom-call(s32[1,16]{1,0:T(1,128)} %bitcast.2, bf16[128,1536]{1,0:T(8,128)(2,1)} %get-tuple-element.5.dq_ref, bf16[4,3,2,16,128]{4,3,2,1,0:T(8,128)(2,1)} %get-tuple-element.6.gkv_ref), custom_call_target="tpu_custom_call" | custom-call | tf_op jit(solution)/shard_map/pallas_call | solution.py:511

commit v5 on v4

--- a/solution.py
+++ b/solution.py
@@ -38,7 +38,7 @@
     idx_ref, k_ref, v_ref, q_ref, g_ref,
     dq_out, gkv,
     kvsend, kv, qb, gb, e_buf, dp_buf, m_buf, stats, stats_in, fin,
-    dq_acc, dqb, dqr, dqs, part, rs_buf, rr_buf, ys_buf, yr_buf, gkv_send,
+    dq_acc, dqb, dqr, dqs, part, rs_buf, rr_buf, ys_buf, gkv_send, zero_send, zero,
     loc_sem, xkv_s, xkv_r, xq_s, xq_r, xg_s, xg_r, y_s, y_r,
     ring_s, ring_r, sib_s, sib_r, join_s, join_r, red_s, red_r, yr_s, yr_r, xo_s, xo_r, xd_s, xd_r,
 ):
@@ -65,6 +65,9 @@
     def xpeer(j):
         return {"blk": ((x + j) % nx) * nz + z}
 
+    def crossed(j):
+        return {"blk": ((x + j) % nx) * nz + z, "uly": (1 - y) * 2 + c}
+
     def send(src, dst, s_sem, r_sem, dev):
         return pltpu.make_async_remote_copy(
             src_ref=src, dst_ref=dst, send_sem=s_sem, recv_sem=r_sem,
@@ -83,7 +86,7 @@
             copy.wait_send()
 
     barrier = pltpu.get_barrier_semaphore()
-    others = [xpeer(j) for j in hop] + [along(1), along(-1), along(2), along(-2), ypeer, sib]
+    others = [xpeer(j) for j in hop] + [crossed(j) for j in hop] + [along(1), along(-1), along(2), along(-2), ypeer, sib]
     for dev in others:
         pl.semaphore_signal(barrier, inc=1, device_id=dev, device_id_type=pl.DeviceIdType.MESH)
 
@@ -392,29 +395,36 @@
         return total
 
     for a in range(2):
-        part[0, a, 0] = total_r(a).astype(BF16)
-    y_last = send(part.at[0, :, 0, 1 - y], yr_buf, yr_s.at[nz], yr_r.at[nz], ypeer)
-    y_last.start()
-
-    def put(h, a, total):
-        if a == 0:
-            total = total * SCALE
+        total = total_r(a) * SCALE if a == 0 else total_r(a)
         total = total.astype(BF16)
-        for xs in range(nx):
-            gkv_send[xs, h, a] = total[xs * rows:(xs + 1) * rows]
+        for ys in range(2):
+            for xs in range(nx):
+                zero_send[xs, ys, a] = total[ys, xs * rows:(xs + 1) * rows]
+    zero_x = [send(zero_send.at[(x + j) % nx, y], zero.at[x, y], xo_s.at[1, j], xo_r.at[1, j], xpeer(j)) for j in hop]
+    zero_x += [send(zero_send.at[(x + j) % nx, 1 - y], zero.at[x, y], xo_s.at[2, j], xo_r.at[2, j], crossed(j))
+               for j in hop + [0]]
+    start(zero_x)
+    zero_own = pltpu.make_async_copy(zero_send.at[x, y], zero.at[x, y], loc_sem.at[5])
+    zero_own.start()
 
     reduce_y(0).wait_recv()
     received(reduce(0, 1))
     for h in range(1, heads):
         for a in range(2):
-            put(h, a, total_s(h, a))
-    y_last.wait_recv()
-    for a in range(2):
-        put(0, a, part[0, a, 0, y].astype(F32) + yr_buf[a].astype(F32))
-    out_x = [send(gkv_send.at[(x + j) % nx], gkv.at[x], xo_s.at[j - 1], xo_r.at[j - 1], xpeer(j)) for j in hop]
+            total = total_s(h, a) * SCALE if a == 0 else total_s(h, a)
+            total = total.astype(BF16)
+            for xs in range(nx):
+                gkv_send[xs, h, a] = total[xs * rows:(xs + 1) * rows]
+    out_x = [send(gkv_send.at[(x + j) % nx, 1:heads], gkv.at[x, 1:heads], xo_s.at[0, j], xo_r.at[0, j], xpeer(j))
+             for j in hop]
     start(out_x)
-    out_own = pltpu.make_async_copy(gkv_send.at[x], gkv.at[x], loc_sem.at[4])
+    out_own = pltpu.make_async_copy(gkv_send.at[x, 1:heads], gkv.at[x, 1:heads], loc_sem.at[4])
     out_own.start()
+    zero_own.wait()
+    received(zero_x)
+    for g in range(nx):
+        for a in range(2):
+            gkv[g, 0, a] = (zero[g, 0, a].astype(F32) + zero[g, 1, a].astype(F32)).astype(BF16)
 
     sent(kv_x)
     for j in hop:
@@ -426,7 +436,8 @@
             sent(ring(kind, s) + reduce(kind, s))
     for slot in range(nz):
         sent([over_y(slot), reduce_y(slot)])
-    sent([y_first, y_last])
+    sent([y_first])
+    sent(zero_x)
     for h in range(heads):
         join(h).wait_send()
     dq_own.wait()
@@ -488,9 +499,10 @@
             vmem((2, half, heads - 1, 2) + slab, BF16),
             vmem((2, half, 2, 2) + slab, BF16),
             vmem((nz, heads - 1, 2) + slab, BF16),
-            vmem((2,) + slab, BF16),
             vmem(compact, BF16),
-            dma((5,)),
+            vmem((nx, 2, 2, rows, HEAD_DIM), BF16),
+            vmem((nx, 2, 2, rows, HEAD_DIM), BF16),
+            dma((6,)),
             dma((nx - 1,)), dma((nx - 1,)),
             dma((nx - 1,)), dma((nx - 1,)),
             dma((nx - 1,)), dma((nx - 1,)),
@@ -500,7 +512,7 @@
             dma((heads,)), dma((heads,)),
             dma((2, 2, half)), dma((2, 2, half)),
             dma((nz + 1,)), dma((nz + 1,)),
-            dma((nx - 1,)), dma((nx - 1,)),
+            dma((3, nx)), dma((3, nx)),
             dma((nx - 1,)), dma((nx - 1,)),
         ],
         compiler_params=pltpu.CompilerParams(

time: 69.8 us -> 69.1 us (0.990)
  the two profiles are of different devices: /device:TPU:16 before, /device:TPU:40 now
where the time goes in v5:
time: 69.1 us; the launch traced here: 69 us
  Pallas kernels  68.3 us (99%)
    pallas_call x1, Pallas kernels, per_device(): pl.pallas_call(functools.partial(kernel, nx, nz, heads, tok, rows), out_s...  66.1 us
    pallas_call x1, Pallas kernels, per_device(): pl.pallas_call(functools.partial(place, nx, heads, tok, rows), out_shape=...  2.27 us

profile of v5, /device:TPU:40, one launch (start us, length us, event | category | flops | bytes accessed | tf_op | source)
XLA Modules:
  0.0 69.0 jit_solution(17296406461563755320)
XLA Ops:
  0.6 66.1 %shard_map.76 = (bf16[128,1536]{1,0:T(8,128)(2,1)}, bf16[4,3,2,16,128]{4,3,2,1,0:T(8,128)(2,1)}) custom-call(s32[1,16]{1,0:T(1,128)} %bitcast.1, bf16[128,1536]{1,0:T(8,128)(2,1)} %k_ref.1, bf16[128,1536]{1,0:T(8,128)(2,1)} %v_ref.1, bf16[128,1536]{1,0:T(8,128)(2,1)} %q_ref.1, bf16[128,1536]{1,0:T(8,128)(2,1)} %g_ref.1), custom_call_target="tpu_custom_call" | custom-call | flops 4831838208 | bytes 2752512 | tf_op jit(solution)/shard_map/pallas_call | solution.py:478
  66.7 2.3 %shard_map.77 = (bf16[128,1536]{1,0:T(8,128)(2,1)}, bf16[128,1536]{1,0:T(8,128)(2,1)}, bf16[128,1536]{1,0:T(8,128)(2,1)}) custom-call(s32[1,16]{1,0:T(1,128)} %bitcast.2, bf16[128,1536]{1,0:T(8,128)(2,1)} %get-tuple-element.5.dq_ref, bf16[4,3,2,16,128]{4,3,2,1,0:T(8,128)(2,1)} %get-tuple-element.6.gkv_ref), custom_call_target="tpu_custom_call" | custom-call | tf_op jit(solution)/shard_map/pallas_call | solution.py:523

commit v6 on v5

--- a/solution.py
+++ b/solution.py
@@ -47,7 +47,7 @@
     hq = nx * tok
     nq = 2 * hq
     nk = 4 * nx * rows
-    tq = min(256, hq)
+    tq = min(512, hq)
     blk = lax.axis_index("blk")
     uly = lax.axis_index("uly")
     x = blk // nz
@@ -201,14 +201,18 @@
         for m in range(half - 1):
             @pl.when(i == 2 * m)
             def _():
-                if m >= 1:
-                    handle(m + 2)
+                if m == 1:
+                    handle(3)
                 received([over_y(2 * m + 2), over_y(2 * m + 3)])
 
         @pl.when(i == 1)
         def _():
             for j in [0] + hop:
                 received(share[j])
+
+        @pl.when(i == 3)
+        def _():
+            handle(4)
 
         def head(h, inner):
             pass1(s, lax.rem(c + later, 2), h)

time: 69.1 us -> 68.7 us (level)
  no operation moved by 1% of the time
where the time goes in v6:
time: 68.7 us; the launch traced here: 68.5 us
  Pallas kernels  67.9 us (99%)
    pallas_call x1, Pallas kernels, per_device(): pl.pallas_call(functools.partial(kernel, nx, nz, heads, tok, rows), out_s...  65.6 us
    pallas_call x1, Pallas kernels, per_device(): pl.pallas_call(functools.partial(place, nx, heads, tok, rows), out_shape=...  2.27 us

profile of v6, /device:TPU:40, one launch (start us, length us, event | category | flops | bytes accessed | tf_op | source)
XLA Modules:
  0.0 68.5 jit_solution(2381796179181558034)
XLA Ops:
  0.6 65.6 %shard_map.76 = (bf16[128,1536]{1,0:T(8,128)(2,1)}, bf16[4,3,2,16,128]{4,3,2,1,0:T(8,128)(2,1)}) custom-call(s32[1,16]{1,0:T(1,128)} %bitcast.1, bf16[128,1536]{1,0:T(8,128)(2,1)} %k_ref.1, bf16[128,1536]{1,0:T(8,128)(2,1)} %v_ref.1, bf16[128,1536]{1,0:T(8,128)(2,1)} %q_ref.1, bf16[128,1536]{1,0:T(8,128)(2,1)} %g_ref.1), custom_call_target="tpu_custom_call" | custom-call | flops 4831838208 | bytes 2752512 | tf_op jit(solution)/shard_map/pallas_call | solution.py:482
  66.2 2.3 %shard_map.77 = (bf16[128,1536]{1,0:T(8,128)(2,1)}, bf16[128,1536]{1,0:T(8,128)(2,1)}, bf16[128,1536]{1,0:T(8,128)(2,1)}) custom-call(s32[1,16]{1,0:T(1,128)} %bitcast.2, bf16[128,1536]{1,0:T(8,128)(2,1)} %get-tuple-element.5.dq_ref, bf16[4,3,2,16,128]{4,3,2,1,0:T(8,128)(2,1)} %get-tuple-element.6.gkv_ref), custom_call_target="tpu_custom_call" | custom-call | tf_op jit(solution)/shard_map/pallas_call | solution.py:527
